TPU v7x, 128 devices: a whole 4x4x4 slice. The times are simulated.
128 devices in a mesh: fsdp: 16 (over z, y_lo, core), tp: 8 (over y_hi, x).
Axes of the slice: x: 4, y: 4 (y_hi: 2, y_lo: 2; y = y_hi * 2 + y_lo), z: 4, core: 2. Of those that a mesh axis runs over, the one named last changes fastest.
Arguments:
- inputs: bfloat16 [65536, 5120], P(('fsdp', 'tp')), may hold values from -6 to 6
- upstream: bfloat16 [65536, 1024], P(('fsdp', 'tp')), may hold values from -6 to 6
- master: float32 [5120, 1024], P('fsdp'), may hold values from -0.078125 to 0.078125
- moment_one: float32 [5120, 1024], P('fsdp'), may hold values from -3 to 3
- moment_two: float32 [5120, 1024], P('fsdp'), may hold values from 0.1 to 2
- hidden_steps: bfloat16 [4, 64, 5120], P(None, 'fsdp'), may hold values from -6 to 6
- key_weight: bfloat16 [5120, 1024], P(None, 'tp'), may hold values from -0.078125 to 0.078125
- queries: bfloat16 [4, 64, 5120], P(None, 'fsdp', 'tp'), may hold values from -18 to 18
- key_cache: bfloat16 [64, 4096, 1024], P('fsdp', None, 'tp'), may hold values from -18 to 18
- value_cache: bfloat16 [64, 4096, 1024], P('fsdp', None, 'tp'), may hold values from -6 to 6
- lengths: int32 [64], P('fsdp'), may hold values from 512 to 4096, as said below
Outputs:
- input_grad: bfloat16 [65536, 5120], P(('fsdp', 'tp'))
- new_master: float32 [5120, 1024], P('fsdp')
- new_moment: float32 [5120, 1024], P('fsdp')
- fresh_kv: bfloat16 [4, 64, 2, 1024], P(None, 'fsdp', None, 'tp')
- attended: bfloat16 [4, 64, 5120], P(None, 'fsdp', 'tp')
Inputs may be any that keep to these rules, and one draw needn't show every extreme that they name: `lengths`: at least one row has a full cache of 4096 slots.
All inputs are finite; a program needn't handle non-finite values.
Results may differ from a plain program's by a relative error of at most 0.0049.
Values may be sent and summed in bfloat16 or wider, within the bound.
A program may use at most 128 MiB of HBM per device.

v0:
```python
import math

import jax
import jax.numpy as jnp
from jax import lax
from jax.sharding import PartitionSpec as P

HD = 128
GROUP = 5


beta_one = 0.9
beta_two = 0.95
learn_rate = 0.004
decay_rate = 0.1
adam_eps = 1e-08
correction_one = 1.0 - 0.9**20
correction_two = 1.0 - 0.95**20


def adamw(master, grad, moment_one, moment_two):
    new_first = beta_one * moment_one + (1.0 - beta_one) * grad
    new_second = beta_two * moment_two + (1.0 - beta_two) * grad * grad
    update = new_first / correction_one / (jnp.sqrt(new_second / correction_two) + adam_eps)
    return (master - learn_rate * (update + decay_rate * master), new_first)


def contract_tokens(left, right):
    return lax.dot_general(
        left, right, (((0,), (0,)), ((), ())), preferred_element_type=jnp.float32
    )


def shards(
    inputs,
    upstream,
    master,
    moment_one,
    moment_two,
    hidden_steps,
    key_weight,
    queries,
    key_cache,
    value_cache,
    lengths,
):
    weight = master.astype(jnp.bfloat16)
    grad_factor = 1.0 / math.sqrt(inputs.shape[0] * lax.axis_size("fsdp") * lax.axis_size("tp"))
    product = lax.dot_general(
        upstream,
        lax.all_gather(weight, "fsdp", axis=0, tiled=True),
        (((1,), (1,)), ((), ())),
        preferred_element_type=jnp.float32,
    )
    input_grad = product.astype(jnp.bfloat16)
    part_cols = inputs
    partial_grad = lax.psum_scatter(
        contract_tokens(part_cols, upstream), "fsdp", scatter_dimension=0, tiled=True
    )
    grad = lax.psum(partial_grad, "tp") * grad_factor
    new_master, new_moment = adamw(master, grad, moment_one, moment_two)
    local_cols = key_weight.shape[1]
    column_start = lax.axis_index("tp") * local_cols
    selected = lax.dynamic_slice_in_dim(new_master, column_start, local_cols, 1).astype(
        jnp.bfloat16
    )
    steps_count, rows_here, model_width = hidden_steps.shape
    flat = hidden_steps.reshape(steps_count * rows_here, model_width)
    part_cols = flat
    value_proj = jnp.dot(
        part_cols,
        lax.all_gather(selected, "fsdp", axis=0, tiled=True),
        preferred_element_type=jnp.float32,
    )
    fresh_keys = (
        jnp.dot(flat, key_weight, preferred_element_type=jnp.float32)
        .astype(jnp.bfloat16)
        .reshape(steps_count, rows_here, local_cols)
    )
    fresh_values = value_proj.astype(jnp.bfloat16).reshape(steps_count, rows_here, local_cols)
    fresh_kv = jnp.stack([fresh_keys, fresh_values], axis=2)
    heads_here = local_cols // HD
    cache_len = key_cache.shape[1]
    scale = 1.0 / math.sqrt(HD)
    query_heads = queries.reshape(steps_count, rows_here, heads_here, GROUP, HD)
    cache_keys = key_cache.reshape(rows_here, cache_len, heads_here, HD)
    cache_values = value_cache.reshape(rows_here, cache_len, heads_here, HD)
    new_keys = fresh_keys.reshape(steps_count, rows_here, heads_here, HD)
    new_values = fresh_values.reshape(steps_count, rows_here, heads_here, HD)
    cache_scores = (
        jnp.einsum("srkgd,rckd->srkgc", query_heads, cache_keys, preferred_element_type=jnp.float32)
        * scale
    )
    fresh_scores = (
        jnp.einsum("srkgd,trkd->srkgt", query_heads, new_keys, preferred_element_type=jnp.float32)
        * scale
    )
    slots = lax.broadcasted_iota(jnp.int32, (1, rows_here, 1, 1, cache_len), 4)
    cache_scores = jnp.where(slots < lengths.reshape(1, rows_here, 1, 1, 1), cache_scores, -1e30)
    later = lax.broadcasted_iota(jnp.int32, (steps_count, 1, 1, 1, steps_count), 4)
    now = lax.broadcasted_iota(jnp.int32, (steps_count, 1, 1, 1, steps_count), 0)
    fresh_scores = jnp.where(later <= now, fresh_scores, -1e30)
    highest = jnp.maximum(jnp.max(cache_scores, axis=-1), jnp.max(fresh_scores, axis=-1))[..., None]
    cache_exp = jnp.exp(cache_scores - highest)
    fresh_exp = jnp.exp(fresh_scores - highest)
    normalizer = jnp.sum(cache_exp, axis=-1, keepdims=True) + jnp.sum(
        fresh_exp, axis=-1, keepdims=True
    )
    cache_prob = (cache_exp / normalizer).astype(jnp.bfloat16)
    fresh_prob = (fresh_exp / normalizer).astype(jnp.bfloat16)
    result = jnp.einsum(
        "srkgc,rckd->srkgd", cache_prob, cache_values, preferred_element_type=jnp.float32
    )
    result = result + jnp.einsum(
        "srkgt,trkd->srkgd", fresh_prob, new_values, preferred_element_type=jnp.float32
    )
    attended = result.reshape(steps_count, rows_here, heads_here * GROUP * HD).astype(jnp.bfloat16)
    return (input_grad, new_master, new_moment, fresh_kv, attended)


def solution(mesh):
    in_specs = (
        P(("fsdp", "tp"), None),
        P(("fsdp", "tp"), None),
        P("fsdp", None),
        P("fsdp", None),
        P("fsdp", None),
        P(None, "fsdp", None),
        P(None, "tp"),
        P(None, "fsdp", "tp"),
        P("fsdp", None, "tp"),
        P("fsdp", None, "tp"),
        P("fsdp"),
    )
    out_specs = (
        P(("fsdp", "tp"), None),
        P("fsdp", None),
        P("fsdp", None),
        P(None, "fsdp", None, "tp"),
        P(None, "fsdp", "tp"),
    )
    return jax.shard_map(shards, mesh=mesh, in_specs=in_specs, out_specs=out_specs, check_vma=False)
```

profile of v0, /device:TPU:1, one launch (start us, length us, event | category | flops | bytes accessed | tf_op | source)
XLA Modules:
  0.0 455.9 jit_solution(2129461601825679674)
XLA Ops:
  7.2 0.0 reduce-scatter.2.cloned.1.call-start
  7.2 12.0 %fusion.33 = f32[5120,1024]{1,0:T(8,128)} fusion(bf16[512,5120]{1,0:T(8,128)(2,1)} %param.11, bf16[512,1024]{1,0:T(8,128)(2,1)} %param.12), kind=kOutput, calls=%fused_computation.40 | convolution fusion | flops 5368709120 | bytes 27262976 | tf_op jit(solution)/shard_map/dot_general | solution.py:29
  19.3 0.0 all-reduce.2.cloned.1.call-start
  19.3 226.3 %reduce-scatter.2.cloned.1.call-done = f32[320,1024]{1,0:T(8,128)} async-done(((f32[5120,1024]{1,0:T(8,128)}), f32[320,1024]{1,0:T(8,128)}) %reduce-scatter.2.cloned.1.call-update) | async-done | bytes 1310736 | tf_op jit(solution)/shard_map/reduce_scatter | solution.py:57
  245.6 0.0 all-gather.5.cloned.1.call-start
  245.7 86.7 %all-reduce.2.cloned.1.call-done = f32[320,1024]{1,0:T(8,128)} async-done(((f32[320,1024]{1,0:T(8,128)}), f32[320,1024]{1,0:T(8,128)}) %all-reduce.2.cloned.1.call-update) | async-done | bytes 1310736 | tf_op jit(solution)/shard_map/psum | solution.py:60
  332.4 4.4 multiply_subtract_fusion
  336.8 1.1 copy-done.1
  337.8 0.7 dynamic-slice_convert_fusion
  338.5 0.0 all-gather.3.cloned.1.call-start
  338.6 0.5 all-gather.3.cloned.1.call-update
  339.2 0.3 convolution_convert_fusion.2
  339.5 0.3 fusion.32
  339.8 0.1 iota_compare_fusion
  339.9 3.8 fusion.31
  343.8 0.5 fusion.6
  344.3 30.8 %all-gather.5.cloned.1.call-done = bf16[5120,128]{1,0:T(8,128)(2,1)} async-done(((bf16[320,128]{1,0:T(8,128)(2,1)}), bf16[5120,128]{1,0:T(8,128)(2,1)}) %all-gather.5.cloned.1.call-update) | async-done | bytes 1310736 | tf_op jit(solution)/shard_map/all_gather | solution.py:72
  375.0 1.7 convolution_convert_fusion.1
  376.8 0.2 fusion.26
  377.0 3.3 fusion.16
  380.3 0.6 copy.38
  380.9 0.6 pad_maximum_fusion
  381.5 57.7 %all-gather.3.cloned.1.call-done = bf16[5120,1024]{1,0:T(8,128)(2,1)} async-done(((bf16[320,1024]{1,0:T(8,128)(2,1)}), bf16[5120,1024]{1,0:T(8,128)(2,1)}) %all-gather.3.cloned.1.call-update) | async-done | bytes 10485776 | tf_op jit(solution)/shard_map/all_gather | solution.py:51
  439.2 10.1 %convolution_convert_fusion = bf16[512,5120]{1,0:T(8,128)(2,1)} fusion(bf16[512,1024]{1,0:T(8,128)(2,1)} %param.12, bf16[5120,1024]{1,0:T(8,128)(2,1)} %all-gather.3.cloned.1.call-done), kind=kOutput, calls=%fused_computation | convolution fusion | flops 5371330560 | bytes 16777216 | tf_op jit(solution)/shard_map/dot_general | solution.py:49
  (25 shorter events, 0.3 us)
Async XLA Ops:
  7.2 332.0 %copy-start = (bf16[5120,128]{1,0:T(8,128)(2,1)S(1)}, bf16[5120,128]{1,0:T(8,128)(2,1)}, u32[]{:S(2)}) copy-start(bf16[5120,128]{1,0:T(8,128)(2,1)} %param.17) | copy-start | bytes 3932164
  7.2 238.4 %reduce-scatter.2.cloned.1.call-start = ((), (), s32[]{:S(2)}) async-start(), calls=%async_computation.2 | async-start | bytes 22282240 | tf_op jit(solution)/shard_map/reduce_scatter | solution.py:57
  19.3 313.1 %copy-start.3 = (f32[320,1024]{1,0:T(8,128)S(1)}, f32[320,1024]{1,0:T(8,128)}, u32[]{:S(2)}) copy-start(f32[320,1024]{1,0:T(8,128)} %param.13) | copy-start | bytes 3932164
  19.3 313.1 %all-reduce.2.cloned.1.call-start = ((), (), s32[]{:S(2)}) async-start(), calls=%async_computation.3 | async-start | bytes 2621440 | tf_op jit(solution)/shard_map/psum | solution.py:60
  245.6 129.4 %all-gather.5.cloned.1.call-start = ((), (), s32[]{:S(2)}) async-start(), calls=%async_computation.4 | async-start | bytes 1392640 | tf_op jit(solution)/shard_map/all_gather | solution.py:72
  245.7 93.5 %copy-start.4 = (bf16[4,4,5120]{2,1,0:T(4,128)(2,1)S(1)}, bf16[4,4,5120]{2,1,0:T(4,128)(2,1)}, u32[]{:S(2)}) copy-start(bf16[4,4,5120]{2,1,0:T(4,128)(2,1)} %param.16) | copy-start | bytes 491524
  336.8 1.1 copy-start.1
  338.5 1.0 copy-start.5
  338.5 100.7 %all-gather.3.cloned.1.call-start = ((), (), s32[]{:S(2)}) async-start(), calls=%async_computation.1 | async-start | bytes 11141120 | tf_op jit(solution)/shard_map/all_gather | solution.py:51
  338.6 1.3 copy-start.6
  339.2 0.7 copy-start.2
Sparse Core Ops, SparseCore 0:
  19.4 226.1 reduce-scatter.1
  248.1 84.2 all-reduce.1
  338.6 36.3 all-gather.4
  377.2 62.0 all-gather.2
where the time goes:
time: 456 us
  waiting for transfers between devices  402 us (88%)
  matrix products  31.6 us (7%)
  between operations  13.9 us (3%)
  other arithmetic  5.68 us (1%)
    reduce_scatter x1, waiting for transfers between devices, shards(): lax.psum_scatter(contract_tokens(part_cols, upstream), 'fsdp', scatter_di...  226 us
    psum x1, waiting for transfers between devices, shards(): grad = lax.psum(partial_grad, 'tp') * grad_factor  86.7 us
    all_gather x1, waiting for transfers between devices, shards(): lax.all_gather(weight, 'fsdp', axis=0, tiled=True)  57.7 us
    all_gather x1, waiting for transfers between devices, shards(): lax.all_gather(selected, 'fsdp', axis=0, tiled=True)  30.8 us
    dot_general x1, matrix products, contract_tokens(): lax.dot_general(left, right, (((0,), (0,)), ((), ())), preferred_element_...  12 us
    dot_general x1, matrix products, shards(): lax.dot_general(upstream, lax.all_gather(weight, 'fsdp', axis=0, tiled=Tr...  10.1 us
  transfers between devices with their start and end apart: 4, of which 4 were waited for; matrix products, arithmetic and copies ran while one was open for 3% of the time, Pallas kernels for 0%

commit v1 on v0

--- a/solution.py
+++ b/solution.py
@@ -1,12 +1,16 @@
+import functools
 import math
 
 import jax
 import jax.numpy as jnp
 from jax import lax
+from jax.experimental import pallas as pl
+from jax.experimental.pallas import tpu as pltpu
 from jax.sharding import PartitionSpec as P
 
 HD = 128
 GROUP = 5
+MESH = pl.DeviceIdType.MESH
 
 
 beta_one = 0.9
@@ -17,6 +21,11 @@
 correction_one = 1.0 - 0.9**20
 correction_two = 1.0 - 0.95**20
 
+A1, B1, C1, A2, B2, C2, A3, B3, C3 = 0, 12, 24, 27, 39, 42, 45, 48, 51
+XS, UT, GX, TP, HS, FR, SEMS = 54, 58, 59, 60, 68, 84, 100
+
+f32, bf16 = jnp.float32, jnp.bfloat16
+
 
 def adamw(master, grad, moment_one, moment_two):
     new_first = beta_one * moment_one + (1.0 - beta_one) * grad
@@ -25,10 +34,385 @@
     return (master - learn_rate * (update + decay_rate * master), new_first)
 
 
-def contract_tokens(left, right):
-    return lax.dot_general(
-        left, right, (((0,), (0,)), ((), ())), preferred_element_type=jnp.float32
-    )
+def learn_kernel(
+    grad_factor,
+    x_hbm,
+    ut,
+    master_hbm,
+    m1_hbm,
+    m2_hbm,
+    hidden,
+    new_master,
+    new_moment,
+    fresh_out,
+    x_own,
+    x_sib,
+    ut_sib,
+    master,
+    m1,
+    m2,
+    ga,
+    gb,
+    gc,
+    r1a,
+    r1b,
+    r1c,
+    s1a,
+    s1b,
+    s1c,
+    r2a,
+    r2b,
+    r2c,
+    s2a,
+    s2b,
+    s2c,
+    r3a,
+    r3b,
+    r3c,
+    gx,
+    gt,
+    gall,
+    wpad,
+    hr,
+    pf,
+    fr,
+    ssem,
+    rsem,
+    lsem,
+):
+    f, t = lax.axis_index("fsdp"), lax.axis_index("tp")
+    z, yl, c = f // 4, (f // 2) % 2, f % 2
+    yh, x = t // 4, t % 4
+    y = yh * 2 + yl
+    sib = (z * 4 + yl * 2 + (1 - c), t)
+
+    def at_x(d):
+        return (x + d) % 4
+
+    def dev_x(d):
+        return (f, yh * 4 + (x + d) % 4)
+
+    def dev_y(d):
+        yy = (y + d) % 4
+        return (z * 4 + (yy % 2) * 2 + c, (yy // 2) * 4 + x)
+
+    def dev_z(d):
+        return (((z + d) % 4) * 4 + yl * 2 + c, t)
+
+    def rcopy(src, dst, n, who):
+        return pltpu.make_async_remote_copy(
+            src_ref=src,
+            dst_ref=dst,
+            send_sem=ssem.at[n],
+            recv_sem=rsem.at[n],
+            device_id=who,
+            device_id_type=MESH,
+        )
+
+    def lanes(zz):
+        return pl.ds(pl.multiple_of(zz * 1280, 1280), 1280)
+
+    x_copies = [
+        pltpu.make_async_copy(
+            x_hbm.at[:, lanes((z + 1 + k) % 4)], x_own.at[:, lanes((z + 1 + k) % 4)], lsem.at[k]
+        )
+        for k in range(4)
+    ]
+    opt_copies = [
+        pltpu.make_async_copy(a, b, lsem.at[4 + i])
+        for i, (a, b) in enumerate([(master_hbm, master), (m1_hbm, m1), (m2_hbm, m2)])
+    ]
+    for cp in x_copies + opt_copies:
+        cp.start()
+
+    barrier = pltpu.get_barrier_semaphore()
+
+    @pl.loop(1, 16)
+    def _(j):
+        pl.semaphore_signal(barrier, 1, device_id=((f + j) % 16, t), device_id_type=MESH)
+
+    @pl.loop(1, 8)
+    def _(j):
+        pl.semaphore_signal(barrier, 1, device_id=(f, (t + j) % 8), device_id_type=MESH)
+
+    pl.semaphore_signal(
+        barrier,
+        1,
+        device_id=(z * 4 + (1 - yl) * 2 + c, (1 - yh) * 4 + x),
+        device_id_type=MESH,
+    )
+    pl.semaphore_wait(barrier, 23)
+
+    ut_copy = rcopy(ut.at[1 - c], ut_sib, UT, sib)
+    ut_copy.start()
+    sib_copies = [
+        rcopy(x_hbm.at[:, lanes((z + 1 + k) % 4)], x_sib.at[:, lanes((z + 1 + k) % 4)], XS + k, sib)
+        for k in range(4)
+    ]
+    for cp in sib_copies:
+        cp.start()
+
+    def hidden_copy(j):
+        to = (f + j) % 16
+        cols = pl.ds(pl.multiple_of((to // 2) * 640, 640), 640)
+        return rcopy(hidden.at[:, cols], hr.at[j], HS + j, (to, t))
+
+    @pl.loop(1, 16)
+    def _(j):
+        hidden_copy(j).start()
+
+    hr[0] = hidden[:, pl.ds(pl.multiple_of((f // 2) * 640, 640), 640)]
+    wpad[...] = jnp.zeros_like(wpad)
+
+    def a1(d, zz, k):
+        return rcopy(
+            ga.at[at_x(d), :, zz], r1a.at[d - 1, :, zz], A1 + (d - 1) * 4 + k, dev_x(d)
+        )
+
+    def b1(d, zz, k):
+        yy = (y + d) % 4
+        return rcopy(
+            gb.at[:, yy // 2, zz, yy % 2], r1b.at[d - 1, :, zz], B1 + (d - 1) * 4 + k, dev_y(d)
+        )
+
+    def c1(d):
+        return rcopy(gc.at[:, :, (z + d) % 4], r1c.at[d - 1], C1 + d - 1, dev_z(d))
+
+    def a2(d, zz, k):
+        yy = (y + d) % 4
+        return rcopy(
+            s1a.at[yy // 2, zz, yy % 2], r2a.at[d - 1, zz], A2 + (d - 1) * 4 + k, dev_y(d)
+        )
+
+    def b2(d):
+        return rcopy(s1b.at[:, (z + d) % 4], r2b.at[d - 1], B2 + d - 1, dev_z(d))
+
+    def c2(d):
+        return rcopy(s1c.at[at_x(d)], r2c.at[d - 1], C2 + d - 1, dev_x(d))
+
+    def a3(d):
+        return rcopy(s2a.at[(z + d) % 4], r3a.at[d - 1], A3 + d - 1, dev_z(d))
+
+    def b3(d):
+        return rcopy(s2b.at[at_x(d)], r3b.at[d - 1], B3 + d - 1, dev_x(d))
+
+    def c3(d):
+        yy = (y + d) % 4
+        return rcopy(s2c.at[yy // 2, yy % 2], r3c.at[d - 1], C3 + d - 1, dev_y(d))
+
+    ut_copy.wait()
+    for k in range(4):
+        zz = (z + 1 + k) % 4
+        x_copies[k].wait()
+        sib_copies[k].wait()
+
+        @pl.loop(0, 4)
+        def _(i):
+            ll, half = i // 2, i % 2
+            cols = pl.ds(pl.multiple_of(zz * 1280 + ll * 640, 640), 640)
+            rows = pl.ds(pl.multiple_of(half * 256, 256), 256)
+            part = jnp.dot(ut[c, rows], x_own[:, cols], preferred_element_type=f32)
+            part += jnp.dot(ut_sib[rows], x_sib[:, cols], preferred_element_type=f32)
+            part = part.astype(bf16)
+            for b in range(4):
+                xx, hh = half * 2 + b // 2, b % 2
+                ga[xx, hh, zz, ll] = part[b * 64 : (b + 1) * 64, 0:256]
+                gb[xx, hh, zz, ll] = part[b * 64 : (b + 1) * 64, 256:512]
+                gc[xx, hh, zz, ll] = part[b * 64 : (b + 1) * 64, 512:640]
+
+        for d in (2, 1, 3):
+            a1(d, zz, k).start()
+            b1(d, zz, k).start()
+        if k < 3:
+            c1(k + 1).start()
+
+    def total(own, others, index):
+        got = own.astype(f32)
+        for d in range(3):
+            got += others[(d,) + index].astype(f32)
+        return got
+
+    for k in range(4):
+        zz = (z + 1 + k) % 4
+        for d in (1, 2, 3):
+            a1(d, zz, k).wait()
+
+        @pl.loop(0, 4)
+        def _(i):
+            hh, ll = i // 2, i % 2
+            s1a[hh, zz, ll] = total(ga[x, hh, zz, ll], r1a, (hh, zz, ll)).astype(bf16)
+
+        for d in (2, 1, 3):
+            a2(d, zz, k).start()
+        for d in (1, 2, 3):
+            b1(d, zz, k).wait()
+
+        @pl.loop(0, 4)
+        def _(i):
+            s1b[i, zz] = total(gb[i, yh, zz, yl], r1b, (i, zz)).astype(bf16)
+
+        if k < 3:
+            b2(k + 1).start()
+    for d in (1, 2, 3):
+        c1(d).wait()
+
+    @pl.loop(0, 16)
+    def _(i):
+        xx, hh, ll = i // 4, (i // 2) % 2, i % 2
+        s1c[xx, hh, ll] = total(gc[xx, hh, z, ll], r1c, (xx, hh, ll)).astype(bf16)
+
+    for d in (2, 1, 3):
+        c2(d).start()
+
+    for k in range(4):
+        zz = (z + 1 + k) % 4
+        for d in (1, 2, 3):
+            a2(d, zz, k).wait()
+        s2a[zz] = total(s1a[yh, zz, yl], r2a, (zz,))
+        if k < 3:
+            a3(k + 1).start()
+    for d in (1, 2, 3):
+        b2(d).wait()
+
+    @pl.loop(0, 4)
+    def _(i):
+        s2b[i] = total(s1b[i, z], r2b, (i,))
+
+    for d in (2, 1, 3):
+        b3(d).start()
+    for d in (1, 2, 3):
+        c2(d).wait()
+
+    @pl.loop(0, 4)
+    def _(i):
+        hh, ll = i // 2, i % 2
+        s2c[hh, ll] = total(s1c[x, hh, ll], r2c, (hh, ll))
+
+    for d in (2, 1, 3):
+        c3(d).start()
+
+    for d in (1, 2, 3):
+        a3(d).wait()
+        b3(d).wait()
+        c3(d).wait()
+    gx[c, :, 0:256] = total(s2a[z], r3a, ()) * grad_factor
+    gx[c, :, 256:512] = total(s2b[x], r3b, ()) * grad_factor
+    gx[c, :, 512:640] = total(s2c[yh, yl], r3c, ()) * grad_factor
+    gx_copy = rcopy(gx.at[c], gx.at[c], GX, sib)
+    gx_copy.start()
+    gx_copy.wait()
+    gt[...] = gx[...].reshape(128, 640).T
+    mine = pl.ds(pl.multiple_of(c * 320, 320), 320)
+    gall[t] = gt[mine, :].astype(bf16)
+
+    def tp_copy(j):
+        return rcopy(gall.at[t], gall.at[t], TP + j, (f, (t + j) % 8))
+
+    @pl.loop(1, 8)
+    def _(j):
+        tp_copy(j).start()
+
+    for cp in opt_copies:
+        cp.wait()
+
+    def update(tt):
+        cols = pl.ds(pl.multiple_of(tt * 128, 128), 128)
+        nm, nf = adamw(master[:, cols], gall[tt].astype(f32), m1[:, cols], m2[:, cols])
+        new_master[:, cols] = nm
+        new_moment[:, cols] = nf
+        return nm
+
+    wpad[mine, :] = update(t).astype(bf16)
+
+    @pl.loop(1, 16)
+    def _(j):
+        hidden_copy(j).wait()
+
+    pf[...] = jnp.dot(
+        hr[...].reshape(256, 640), wpad[...], preferred_element_type=f32
+    ).reshape(16, 16, 128)
+
+    def fresh_copy(j):
+        return rcopy(pf.at[j], fr.at[j], FR + j, ((f + 16 - j) % 16, t))
+
+    @pl.loop(1, 16)
+    def _(j):
+        fresh_copy(j).start()
+
+    @pl.loop(1, 8)
+    def _(j):
+        tp_copy(j).wait()
+        update((t + 8 - j) % 8)
+
+    @pl.loop(1, 16)
+    def _(j):
+        fresh_copy(j).wait()
+
+    fr[0] = pf[0]
+    fresh_out[...] = jnp.sum(fr[...], axis=0)
+
+
+def learn(inputs, upstream, master, m1, m2, flat, grad_factor):
+    tokens, width = inputs.shape
+    ut = upstream.reshape(tokens, 2, 4, 2, 64).transpose(3, 2, 1, 4, 0).reshape(2, 512, tokens)
+    hbm = pl.BlockSpec(memory_space=pl.ANY)
+    vmem = pl.BlockSpec(memory_space=pltpu.VMEM)
+    shape = jax.ShapeDtypeStruct
+    V = pltpu.VMEM
+    scratch = [
+        V((512, 5120), bf16),
+        V((512, 5120), bf16),
+        V((512, 512), bf16),
+        V((320, 1024), f32),
+        V((320, 1024), f32),
+        V((320, 1024), f32),
+        V((4, 2, 4, 2, 64, 256), bf16),
+        V((4, 2, 4, 2, 64, 256), bf16),
+        V((4, 2, 4, 2, 64, 128), bf16),
+        V((3, 2, 4, 2, 64, 256), bf16),
+        V((3, 4, 4, 64, 256), bf16),
+        V((3, 4, 2, 2, 64, 128), bf16),
+        V((2, 4, 2, 64, 256), bf16),
+        V((4, 4, 64, 256), bf16),
+        V((4, 2, 2, 64, 128), bf16),
+        V((3, 4, 64, 256), bf16),
+        V((3, 4, 64, 256), bf16),
+        V((3, 2, 2, 64, 128), bf16),
+        V((4, 64, 256), f32),
+        V((4, 64, 256), f32),
+        V((2, 2, 64, 128), f32),
+        V((3, 64, 256), f32),
+        V((3, 64, 256), f32),
+        V((3, 64, 128), f32),
+        V((2, 64, 640), f32),
+        V((640, 128), f32),
+        V((8, 320, 128), bf16),
+        V((640, 128), bf16),
+        V((16, 16, 640), bf16),
+        V((16, 16, 128), f32),
+        V((16, 16, 128), f32),
+        pltpu.SemaphoreType.DMA((SEMS,)),
+        pltpu.SemaphoreType.DMA((SEMS,)),
+        pltpu.SemaphoreType.DMA((7,)),
+    ]
+    return pl.pallas_call(
+        functools.partial(learn_kernel, grad_factor),
+        out_shape=(
+            shape((320, 1024), f32),
+            shape((320, 1024), f32),
+            shape((16, 128), f32),
+        ),
+        in_specs=[hbm, vmem, hbm, hbm, hbm, vmem],
+        out_specs=[vmem, vmem, vmem],
+        scratch_shapes=scratch,
+        name="learn",
+        cost_estimate=pl.CostEstimate(
+            flops=60_000_000_000, bytes_accessed=160_000_000, transcendentals=0
+        ),
+        compiler_params=pltpu.CompilerParams(
+            collective_id=0, has_side_effects=True, vmem_limit_bytes=56 << 20
+        ),
+    )(inputs, ut, master, m1, m2, flat)
 
 
 def shards(
@@ -46,32 +430,20 @@
 ):
     weight = master.astype(jnp.bfloat16)
     grad_factor = 1.0 / math.sqrt(inputs.shape[0] * lax.axis_size("fsdp") * lax.axis_size("tp"))
+    steps_count, rows_here, model_width = hidden_steps.shape
+    flat = hidden_steps.reshape(steps_count * rows_here, model_width)
+    gathered = lax.all_gather(weight, "fsdp", axis=0, tiled=True)
+    new_master, new_moment, value_proj = learn(
+        inputs, upstream, master, moment_one, moment_two, flat, grad_factor
+    )
     product = lax.dot_general(
         upstream,
-        lax.all_gather(weight, "fsdp", axis=0, tiled=True),
+        gathered,
         (((1,), (1,)), ((), ())),
         preferred_element_type=jnp.float32,
     )
     input_grad = product.astype(jnp.bfloat16)
-    part_cols = inputs
-    partial_grad = lax.psum_scatter(
-        contract_tokens(part_cols, upstream), "fsdp", scatter_dimension=0, tiled=True
-    )
-    grad = lax.psum(partial_grad, "tp") * grad_factor
-    new_master, new_moment = adamw(master, grad, moment_one, moment_two)
     local_cols = key_weight.shape[1]
-    column_start = lax.axis_index("tp") * local_cols
-    selected = lax.dynamic_slice_in_dim(new_master, column_start, local_cols, 1).astype(
-        jnp.bfloat16
-    )
-    steps_count, rows_here, model_width = hidden_steps.shape
-    flat = hidden_steps.reshape(steps_count * rows_here, model_width)
-    part_cols = flat
-    value_proj = jnp.dot(
-        part_cols,
-        lax.all_gather(selected, "fsdp", axis=0, tiled=True),
-        preferred_element_type=jnp.float32,
-    )
     fresh_keys = (
         jnp.dot(flat, key_weight, preferred_element_type=jnp.float32)
         .astype(jnp.bfloat16)

time: 456 us -> 140 us (0.31)
  waiting for transfers between devices: 402 us -> 0.02 us
  Pallas kernels: 0 us -> 99.6 us
  matrix products: 31.6 us -> 16 us
    reduce_scatter x1 -> x0, waiting for transfers between devices: 226 us -> none  [shards(): lax.psum_scatter(contract_tokens(part_cols, upstream), 'fsdp', scatter_di...]
    pallas_call x0 -> x1, Pallas kernels: none -> 99.6 us  [learn(): pl.pallas_call(functools.partial(learn_kernel, grad_factor), out_shape=(s...]
    all_gather x2 -> x1, waiting for transfers between devices: 88.5 us -> 0.01 us  [shards(): gathered = lax.all_gather(weight, 'fsdp', axis=0, tiled=True)]
    psum x1 -> x0, waiting for transfers between devices: 86.7 us -> none  [shards(): grad = lax.psum(partial_grad, 'tp') * grad_factor]
    dot_general x3 -> x1, matrix products: 23.8 us -> 10.2 us  [shards(): lax.dot_general(upstream, gathered, (((1,), (1,)), ((), ())), preferred_e...]
  transfers between devices with their start and end apart: 4 -> 1, of which waited for: 4 -> 0; matrix products, arithmetic and copies ran while one was open for 3% -> 8% of each run, Pallas kernels for 0% -> 71%
where the time goes in v1:
time: 140 us
  Pallas kernels  99.6 us (71%)
  matrix products  16 us (11%)
  between operations  14.2 us (10%)
  local copies, waits for them, and re-layouts  5.89 us (4%)
  other arithmetic  4.38 us (3%)
    pallas_call x1, Pallas kernels, learn(): pl.pallas_call(functools.partial(learn_kernel, grad_factor), out_shape=(s...  99.6 us
    dot_general x1, matrix products, shards(): lax.dot_general(upstream, gathered, (((1,), (1,)), ((), ())), preferred_e...  10.2 us
    dot_general x1, matrix products, shards(): jnp.einsum('srkgd,rckd->srkgc', query_heads, cache_keys, preferred_elemen...  3.91 us
    unnamed x21, local copies, waits for them, and re-layouts  3.43 us
  transfers between devices with their start and end apart: 1, of which 0 were waited for; matrix products, arithmetic and copies ran while one was open for 8% of the time, Pallas kernels for 71%

profile of v1, /device:TPU:1, one launch (start us, length us, event | category | flops | bytes accessed | tf_op | source)
XLA Modules:
  0.0 140.1 jit_solution(8378263479433867313)
XLA Ops:
  7.2 0.0 copy-start
  7.2 0.0 all-gather.2.cloned.1.call-start
  7.2 2.4 %convert_element_type.30 = bf16[320,1024]{1,0:T(8,128)(2,1)} convert(f32[320,1024]{1,0:T(8,128)} %master_hbm.1) | non-fusion elementwise | flops 327680 | bytes 1966080 | tf_op jit(solution)/shard_map/convert_element_type | solution.py:431
  9.6 0.0 all-gather.2.cloned.1.call-update
  9.7 0.5 copy.24
  10.2 0.0 copy-start.5
  10.2 1.1 copy.25
  11.3 0.7 reshape.125.hidden
  12.0 99.6 %learn.1 = (f32[320,1024]{1,0:T(8,128)}, f32[320,1024]{1,0:T(8,128)}, f32[16,128]{1,0:T(8,128)}) custom-call(bf16[512,5120]{1,0:T(8,128)(2,1)} %x_hbm.1, bf16[2,512,512]{2,1,0:T(8,128)(2,1)} %bitcast.71, f32[320,1024]{1,0:T(8,128)} %master_hbm.1, f32[320,1024]{1,0:T(8,128)} %m1_hbm.1, f32[320,1024]{1,0:T(8,128)} %m2_hbm.1, bf16[16,5120]{1,0:T(8,128)(2,1)} %reshape.125.hidden), custom_call_target="tpu_custom_call" | custom-call | flops 60000002048 | bytes 160000000 | tf_op jit(solution)/shard_map/learn/pallas_call | solution.py:398
  111.6 0.7 convert_element_type.33
  112.3 0.3 convolution_convert_fusion.1
  112.7 0.3 fusion.32
  113.0 0.1 iota_compare_fusion
  113.1 0.0 copy-start.8
  113.1 3.9 %fusion.31 = (f32[4,4,5]{2,0,1:T(4,128)S(1)}, f32[4,4,1,5,4096]{4,3,0,1,2:T(8,128)S(1)}) fusion(bf16[4,4,5,128]{3,2,1,0:T(8,128)(2,1)S(1)} %reshape.126, bf16[4,4096,128]{2,1,0:T(8,128)(2,1)} %param.19, pred[4,4096]{1,0:T(4,128)(4,1)S(1)} %iota_compare_fusion), kind=kOutput, calls=%fused_computation.34 | convolution fusion | flops 84869040 | bytes 5542208 | tf_op jit(solution)/shard_map/srkgd,rckd->srkgc/dot_general | solution.py:463
  117.0 0.5 fusion.6
  117.5 0.2 fusion.26
  117.8 1.1 fusion.16
  118.9 0.6 copy.41
  119.5 0.6 pad_maximum_fusion
  120.2 10.2 %convolution_convert_fusion = bf16[512,5120]{1,0:T(8,128)(2,1)} fusion(bf16[512,1024]{1,0:T(8,128)(2,1)} %param.12, bf16[5120,1024]{1,0:T(8,128)(2,1)} %all-gather.2.cloned.1.call-done), kind=kOutput, calls=%fused_computation | convolution fusion | flops 5371330560 | bytes 16777216 | tf_op jit(solution)/shard_map/dot_general | solution.py:439
  130.4 1.1 copy.58
  131.4 0.7 copy-done.1
  132.2 1.1 copy.59
  (23 shorter events, 0.2 us)
Async XLA Ops:
  7.2 105.1 %copy-start = (bf16[5120,128]{1,0:T(8,128)(2,1)S(1)}, bf16[5120,128]{1,0:T(8,128)(2,1)}, u32[]{:S(2)}) copy-start(bf16[5120,128]{1,0:T(8,128)(2,1)} %param.17) | copy-start | bytes 3932164
  7.2 2.5 %copy-start.3 = (bf16[512,1024]{1,0:T(8,128)(2,1)S(1)}, bf16[512,1024]{1,0:T(8,128)(2,1)}, u32[]{:S(2)}) copy-start(bf16[512,1024]{1,0:T(8,128)(2,1)} %param.12) | copy-start | bytes 3145732
  7.2 113.0 %all-gather.2.cloned.1.call-start = ((), (), s32[]{:S(2)}) async-start(), calls=%async_computation | async-start | bytes 11141120 | tf_op jit(solution)/shard_map/all_gather | solution.py:435
  10.2 1.1 copy-start.5
  12.0 100.3 %copy-start.4 = (bf16[16,5120]{1,0:T(8,128)(2,1)S(1)}, bf16[16,5120]{1,0:T(8,128)(2,1)}, u32[]{:S(2)}) copy-start(bf16[16,5120]{1,0:T(8,128)(2,1)} %reshape.125.hidden) | copy-start | bytes 491524
  12.0 100.6 %copy-start.6 = (bf16[4,4,640]{2,1,0:T(4,128)(2,1)S(1)}, bf16[4,4,640]{2,1,0:T(4,128)(2,1)}, u32[]{:S(2)}) copy-start(bf16[4,4,640]{2,1,0:T(4,128)(2,1)} %param.18) | copy-start | bytes 61444
  12.0 100.9 %copy-start.7 = (s32[4]{0:T(128)S(1)}, s32[4]{0:T(128)}, u32[]{:S(2)}) copy-start(s32[4]{0:T(128)} %param.21) | copy-start | bytes 52
  113.1 4.7 %copy-start.8 = (bf16[4,4096,128]{2,1,0:T(8,128)(2,1)S(1)}, bf16[4,4096,128]{2,1,0:T(8,128)(2,1)}, u32[]{:S(2)}) copy-start(bf16[4,4096,128]{2,1,0:T(8,128)(2,1)} %param.20) | copy-start | bytes 12582916
  120.2 10.2 %copy-start.2 = (f32[320,1024]{1,0:T(8,128)S(1)}, f32[320,1024]{1,0:T(8,128)}, u32[]{:S(2)}) copy-start(f32[320,1024]{1,0:T(8,128)} %get-tuple-element.26) | copy-start | bytes 3932164
  130.4 1.8 %copy-start.1 = (f32[320,1024]{1,0:T(8,128)S(1)}, f32[320,1024]{1,0:T(8,128)}, u32[]{:S(2)}) copy-start(f32[320,1024]{1,0:T(8,128)} %get-tuple-element.27) | copy-start | bytes 3932164
Sparse Core Ops, SparseCore 0:
  10.3 103.3 all-gather.1

commit v2 on v1

--- a/solution.py
+++ b/solution.py
@@ -22,7 +22,9 @@
 correction_two = 1.0 - 0.95**20
 
 A1, B1, C1, A2, B2, C2, A3, B3, C3 = 0, 12, 24, 27, 39, 42, 45, 48, 51
-XS, UT, GX, TP, HS, FR, SEMS = 54, 58, 59, 60, 68, 84, 100
+XS, UT, GX, TP, HS, FR = 54, 58, 59, 60, 68, 84
+WZ, WY, WX, WS, SEMS = 100, 106, 122, 143, 151
+WHOLE, QUARTER = 192, 32
 
 f32, bf16 = jnp.float32, jnp.bfloat16
 
@@ -37,14 +39,29 @@
 def learn_kernel(
     grad_factor,
     x_hbm,
-    ut,
+    u,
     master_hbm,
     m1_hbm,
     m2_hbm,
     hidden,
+    kw_hbm,
+    queries,
+    k_hbm,
+    v_hbm,
+    lengths,
+    grad_hbm,
     new_master,
     new_moment,
     fresh_out,
+    attended,
+    ut,
+    wall,
+    kw,
+    keys,
+    values,
+    qf,
+    acc,
+    fprob,
     x_own,
     x_sib,
     ut_sib,
@@ -122,7 +139,11 @@
         pltpu.make_async_copy(a, b, lsem.at[4 + i])
         for i, (a, b) in enumerate([(master_hbm, master), (m1_hbm, m1), (m2_hbm, m2)])
     ]
-    for cp in x_copies + opt_copies:
+    attn_copies = [
+        pltpu.make_async_copy(a, b, lsem.at[7 + i])
+        for i, (a, b) in enumerate([(kw_hbm, kw), (k_hbm, keys), (v_hbm, values)])
+    ]
+    for cp in opt_copies[:1] + x_copies + attn_copies + opt_copies[1:]:
         cp.start()
 
     barrier = pltpu.get_barrier_semaphore()
@@ -141,6 +162,14 @@
         device_id=(z * 4 + (1 - yl) * 2 + c, (1 - yh) * 4 + x),
         device_id_type=MESH,
     )
+    own = z * 2 + yl
+    opt_copies[0].wait()
+    wall[own, c] = master[...].astype(bf16)
+    for tt in range(8):
+        block = u[:, tt * 128 : (tt + 1) * 128].T
+        place = ((tt % 4) * 2 + tt // 4) * 64
+        ut[0, place : place + 64] = block[0:64]
+        ut[1, place : place + 64] = block[64:128]
     pl.semaphore_wait(barrier, 23)
 
     ut_copy = rcopy(ut.at[1 - c], ut_sib, UT, sib)
@@ -151,6 +180,58 @@
     ]
     for cp in sib_copies:
         cp.start()
+
+    quarter = WHOLE + x * QUARTER
+
+    def wz(d, part):
+        rows = (pl.ds(0, WHOLE), pl.ds(pl.multiple_of(quarter, 32), QUARTER))[part]
+        piece = wall.at[own, c, rows]
+        return rcopy(piece, piece, WZ + (d - 1) * 2 + part, dev_z(d))
+
+    def wy(dz, way, part):
+        first = (way * (WHOLE // 2), pl.multiple_of(quarter + way * (QUARTER // 2), 16))[part]
+        rows = pl.ds(first, (WHOLE // 2, QUARTER // 2)[part])
+        piece = wall.at[((z + dz) % 4) * 2 + yl, c, rows]
+        return rcopy(piece, piece, WY + (dz * 2 + way) * 2 + part, dev_y(1 if way == 0 else 3))
+
+    def wx(dz, other, d):
+        ll = 1 - yl if other else yl
+        rows = pl.ds(pl.multiple_of(quarter, 32), QUARTER)
+        piece = wall.at[((z + dz) % 4) * 2 + ll, c, rows]
+        return rcopy(piece, piece, WX + (other * 3 + dz + other - 1) * 3 + d - 1, dev_x(d))
+
+    def ws(dz, other):
+        ll = 1 - yl if other else yl
+        piece = wall.at[((z + dz) % 4) * 2 + ll, c]
+        return rcopy(piece, piece, WS + other * 4 + dz, sib)
+
+    def grad_out(dz, other):
+        ll = 1 - yl if other else yl
+        cols = pl.ds(pl.multiple_of((((z + dz) % 4) * 2 + ll) * 640, 640), 640)
+        return pltpu.make_async_copy(
+            x_own.at[:, cols], grad_hbm.at[:, cols], lsem.at[10 + other * 4 + dz]
+        )
+
+    def input_grads(other):
+        @pl.loop(0, 4)
+        def _(dz):
+            ll = 1 - yl if other else yl
+            ss = ((z + dz) % 4) * 2 + ll
+            cols = pl.ds(pl.multiple_of(ss * 640, 640), 640)
+            x_own[:, cols] = lax.dot_general(
+                u[...],
+                wall[ss].reshape(640, 1024),
+                (((1,), (1,)), ((), ())),
+                preferred_element_type=f32,
+            ).astype(bf16)
+            grad_out(dz, other).start()
+
+    for d in (2, 1, 3):
+        for part in range(2):
+            wz(d, part).start()
+    for way in range(2):
+        for part in range(2):
+            wy(0, way, part).start()
 
     def hidden_copy(j):
         to = (f + j) % 16
@@ -226,6 +307,52 @@
         if k < 3:
             c1(k + 1).start()
 
+    ws(0, 0).start()
+
+    attn_copies[0].wait()
+    fresh_keys = jnp.dot(hidden[...], kw[...], preferred_element_type=f32).astype(bf16)
+    fresh_out[0] = fresh_keys
+    qf[...] = jnp.zeros_like(qf)
+    for step in range(4):
+        for g in range(GROUP):
+            qf[:, step * GROUP + g] = queries[step, :, g * HD : (g + 1) * HD].astype(f32)
+    attn_copies[1].wait()
+    attn_copies[2].wait()
+    scale = 1.0 / math.sqrt(HD)
+    nt = (((1,), (1,)), ((), ()))
+
+    @pl.loop(0, 4)
+    def _(r):
+        q = qf[r].astype(bf16)
+        scores = lax.dot_general(q, keys[r], nt, preferred_element_type=f32) * scale
+        slots = lax.broadcasted_iota(jnp.int32, (32, 4096), 1)
+        scores = jnp.where(slots < lengths[r], scores, -1e30)
+        extra = lax.dot_general(q, fresh_out[0], nt, preferred_element_type=f32) * scale
+        line = lax.broadcasted_iota(jnp.int32, (32, 16), 0)
+        item = lax.broadcasted_iota(jnp.int32, (32, 16), 1)
+        seen = ((item & 3) == r) & ((item >> 2) * GROUP <= line)
+        extra = jnp.where(seen, extra, -1e30)
+        highest = jnp.maximum(
+            jnp.max(scores, axis=1, keepdims=True), jnp.max(extra, axis=1, keepdims=True)
+        )
+        scores = jnp.exp(scores - highest)
+        extra = jnp.exp(extra - highest)
+        norm = 1.0 / (
+            jnp.sum(scores, axis=1, keepdims=True) + jnp.sum(extra, axis=1, keepdims=True)
+        )
+        fprob[r] = (extra * norm).astype(bf16)
+        acc[r] = jnp.dot((scores * norm).astype(bf16), values[r], preferred_element_type=f32)
+
+    for d in (1, 3, 2):
+        for part in range(2):
+            wz(d, part).wait()
+    for dz in (1, 2, 3):
+        for way in range(2):
+            for part in range(2):
+                wy(dz, way, part).start()
+        for d in (2, 1, 3):
+            wx(dz, 0, d).start()
+
     def total(own, others, index):
         got = own.astype(f32)
         for d in range(3):
@@ -263,6 +390,13 @@
 
     for d in (2, 1, 3):
         c2(d).start()
+
+    for dz in range(4):
+        for way in range(2):
+            for part in range(2):
+                wy(dz, way, part).wait()
+        for d in (2, 1, 3):
+            wx(dz, 1, d).start()
 
     for k in range(4):
         zz = (z + 1 + k) % 4
@@ -290,6 +424,14 @@
 
     for d in (2, 1, 3):
         c3(d).start()
+
+    for dz in (1, 2, 3):
+        for d in (1, 2, 3):
+            wx(dz, 0, d).wait()
+        ws(dz, 0).start()
+    for dz in range(4):
+        ws(dz, 0).wait()
+    input_grads(0)
 
     for d in (1, 2, 3):
         a3(d).wait()
@@ -312,7 +454,7 @@
     def _(j):
         tp_copy(j).start()
 
-    for cp in opt_copies:
+    for cp in opt_copies[1:]:
         cp.wait()
 
     def update(tt):
@@ -339,6 +481,11 @@
     def _(j):
         fresh_copy(j).start()
 
+    for dz in range(4):
+        for d in (1, 2, 3):
+            wx(dz, 1, d).wait()
+        ws(dz, 1).start()
+
     @pl.loop(1, 8)
     def _(j):
         tp_copy(j).wait()
@@ -349,17 +496,41 @@
         fresh_copy(j).wait()
 
     fr[0] = pf[0]
-    fresh_out[...] = jnp.sum(fr[...], axis=0)
-
-
-def learn(inputs, upstream, master, m1, m2, flat, grad_factor):
-    tokens, width = inputs.shape
-    ut = upstream.reshape(tokens, 2, 4, 2, 64).transpose(3, 2, 1, 4, 0).reshape(2, 512, tokens)
+    fresh_out[1] = jnp.sum(fr[...], axis=0).astype(bf16)
+
+    @pl.loop(0, 4)
+    def _(r):
+        acc[r] += jnp.dot(fprob[r], fresh_out[1], preferred_element_type=f32)
+
+    for step in range(4):
+        for g in range(GROUP):
+            attended[step, :, g * HD : (g + 1) * HD] = acc[:, step * GROUP + g].astype(bf16)
+
+    for dz in range(4):
+        ws(dz, 1).wait()
+    input_grads(1)
+    for other in range(2):
+        for dz in range(4):
+            grad_out(dz, other).wait()
+
+
+def learn(
+    inputs, upstream, master, m1, m2, flat, key_weight, queries, keys, values, lengths, grad_factor
+):
     hbm = pl.BlockSpec(memory_space=pl.ANY)
     vmem = pl.BlockSpec(memory_space=pltpu.VMEM)
+    smem = pl.BlockSpec(memory_space=pltpu.SMEM)
     shape = jax.ShapeDtypeStruct
     V = pltpu.VMEM
     scratch = [
+        V((2, 512, 512), bf16),
+        V((8, 2, 320, 1024), bf16),
+        V((5120, 128), bf16),
+        V((4, 4096, 128), bf16),
+        V((4, 4096, 128), bf16),
+        V((4, 32, 128), f32),
+        V((4, 32, 128), f32),
+        V((4, 32, 16), bf16),
         V((512, 5120), bf16),
         V((512, 5120), bf16),
         V((512, 512), bf16),
@@ -393,26 +564,28 @@
         V((16, 16, 128), f32),
         pltpu.SemaphoreType.DMA((SEMS,)),
         pltpu.SemaphoreType.DMA((SEMS,)),
-        pltpu.SemaphoreType.DMA((7,)),
+        pltpu.SemaphoreType.DMA((18,)),
     ]
     return pl.pallas_call(
         functools.partial(learn_kernel, grad_factor),
         out_shape=(
+            shape((512, 5120), bf16),
             shape((320, 1024), f32),
             shape((320, 1024), f32),
-            shape((16, 128), f32),
+            shape((2, 16, 128), bf16),
+            shape((4, 4, 640), bf16),
         ),
-        in_specs=[hbm, vmem, hbm, hbm, hbm, vmem],
-        out_specs=[vmem, vmem, vmem],
+        in_specs=[hbm, vmem, hbm, hbm, hbm, vmem, hbm, vmem, hbm, hbm, smem],
+        out_specs=[hbm, vmem, vmem, vmem, vmem],
         scratch_shapes=scratch,
         name="learn",
         cost_estimate=pl.CostEstimate(
             flops=60_000_000_000, bytes_accessed=160_000_000, transcendentals=0
         ),
         compiler_params=pltpu.CompilerParams(
-            collective_id=0, has_side_effects=True, vmem_limit_bytes=56 << 20
+            collective_id=0, has_side_effects=True, vmem_limit_bytes=60 << 20
         ),
-    )(inputs, ut, master, m1, m2, flat)
+    )(inputs, upstream, master, m1, m2, flat, key_weight, queries, keys, values, lengths)
 
 
 def shards(
@@ -428,65 +601,23 @@
     value_cache,
     lengths,
 ):
-    weight = master.astype(jnp.bfloat16)
     grad_factor = 1.0 / math.sqrt(inputs.shape[0] * lax.axis_size("fsdp") * lax.axis_size("tp"))
-    steps_count, rows_here, model_width = hidden_steps.shape
-    flat = hidden_steps.reshape(steps_count * rows_here, model_width)
-    gathered = lax.all_gather(weight, "fsdp", axis=0, tiled=True)
-    new_master, new_moment, value_proj = learn(
-        inputs, upstream, master, moment_one, moment_two, flat, grad_factor
+    flat = hidden_steps.reshape(16, 5120)
+    input_grad, new_master, new_moment, fresh, attended = learn(
+        inputs,
+        upstream,
+        master,
+        moment_one,
+        moment_two,
+        flat,
+        key_weight,
+        queries,
+        key_cache,
+        value_cache,
+        lengths,
+        grad_factor,
     )
-    product = lax.dot_general(
-        upstream,
-        gathered,
-        (((1,), (1,)), ((), ())),
-        preferred_element_type=jnp.float32,
-    )
-    input_grad = product.astype(jnp.bfloat16)
-    local_cols = key_weight.shape[1]
-    fresh_keys = (
-        jnp.dot(flat, key_weight, preferred_element_type=jnp.float32)
-        .astype(jnp.bfloat16)
-        .reshape(steps_count, rows_here, local_cols)
-    )
-    fresh_values = value_proj.astype(jnp.bfloat16).reshape(steps_count, rows_here, local_cols)
-    fresh_kv = jnp.stack([fresh_keys, fresh_values], axis=2)
-    heads_here = local_cols // HD
-    cache_len = key_cache.shape[1]
-    scale = 1.0 / math.sqrt(HD)
-    query_heads = queries.reshape(steps_count, rows_here, heads_here, GROUP, HD)
-    cache_keys = key_cache.reshape(rows_here, cache_len, heads_here, HD)
-    cache_values = value_cache.reshape(rows_here, cache_len, heads_here, HD)
-    new_keys = fresh_keys.reshape(steps_count, rows_here, heads_here, HD)
-    new_values = fresh_values.reshape(steps_count, rows_here, heads_here, HD)
-    cache_scores = (
-        jnp.einsum("srkgd,rckd->srkgc", query_heads, cache_keys, preferred_element_type=jnp.float32)
-        * scale
-    )
-    fresh_scores = (
-        jnp.einsum("srkgd,trkd->srkgt", query_heads, new_keys, preferred_element_type=jnp.float32)
-        * scale
-    )
-    slots = lax.broadcasted_iota(jnp.int32, (1, rows_here, 1, 1, cache_len), 4)
-    cache_scores = jnp.where(slots < lengths.reshape(1, rows_here, 1, 1, 1), cache_scores, -1e30)
-    later = lax.broadcasted_iota(jnp.int32, (steps_count, 1, 1, 1, steps_count), 4)
-    now = lax.broadcasted_iota(jnp.int32, (steps_count, 1, 1, 1, steps_count), 0)
-    fresh_scores = jnp.where(later <= now, fresh_scores, -1e30)
-    highest = jnp.maximum(jnp.max(cache_scores, axis=-1), jnp.max(fresh_scores, axis=-1))[..., None]
-    cache_exp = jnp.exp(cache_scores - highest)
-    fresh_exp = jnp.exp(fresh_scores - highest)
-    normalizer = jnp.sum(cache_exp, axis=-1, keepdims=True) + jnp.sum(
-        fresh_exp, axis=-1, keepdims=True
-    )
-    cache_prob = (cache_exp / normalizer).astype(jnp.bfloat16)
-    fresh_prob = (fresh_exp / normalizer).astype(jnp.bfloat16)
-    result = jnp.einsum(
-        "srkgc,rckd->srkgd", cache_prob, cache_values, preferred_element_type=jnp.float32
-    )
-    result = result + jnp.einsum(
-        "srkgt,trkd->srkgd", fresh_prob, new_values, preferred_element_type=jnp.float32
-    )
-    attended = result.reshape(steps_count, rows_here, heads_here * GROUP * HD).astype(jnp.bfloat16)
+    fresh_kv = fresh.reshape(2, 4, 4, 128).transpose(1, 2, 0, 3)
     return (input_grad, new_master, new_moment, fresh_kv, attended)
 
 

time: 140 us -> 107 us (0.76)
  matrix products: 16 us -> 0 us
  between operations: 14.2 us -> 0.64 us
  local copies, waits for them, and re-layouts: 5.89 us -> 11.7 us
  Pallas kernels: 99.6 us -> 94.1 us
  other arithmetic: 4.38 us -> 0 us
    dot_general x6 -> x0, matrix products: 16 us -> none  [the longest x1 10.2 us: shards(): lax.dot_general(upstream, gathered, (((1,), (1,)), ((), ())), preferred_e...]
    pallas_call x1, Pallas kernels: 99.6 us -> 94.1 us  [learn(): pl.pallas_call(functools.partial(learn_kernel, grad_factor), out_shape=(s...]
    unnamed x21 -> x10, local copies, waits for them, and re-layouts: 3.43 us -> 8.74 us
    convert_element_type x2 -> x0, other arithmetic: 3.1 us -> none  [the longest x1 2.4 us: shards(): weight = master.astype(jnp.bfloat16)]
    reshape x1 -> x2, local copies, waits for them, and re-layouts: 0.71 us -> 2.93 us  [the longest x1 1.62 us: shards(): flat = hidden_steps.reshape(16, 5120)]
  transfers between devices with their start and end apart: 1 -> 0, of which waited for: 0 -> 0; matrix products, arithmetic and copies ran while one was open for 8% -> 0% of each run, Pallas kernels for 71% -> 0%
where the time goes in v2:
time: 107 us; the launch traced here: 106 us
  Pallas kernels  94.1 us (88%)
  local copies, waits for them, and re-layouts  11.7 us (11%)
    pallas_call x1, Pallas kernels, learn(): pl.pallas_call(functools.partial(learn_kernel, grad_factor), out_shape=(s...  94.1 us
    unnamed x10, local copies, waits for them, and re-layouts  8.74 us

profile of v2, /device:TPU:1, one launch (start us, length us, event | category | flops | bytes accessed | tf_op | source)
XLA Modules:
  0.0 106.4 jit_solution(11832933773614967404)
XLA Ops:
  0.6 1.6 %reshape.16.hidden = bf16[16,5120]{1,0:T(8,128)(2,1)} reshape(bf16[4,4,5120]{2,1,0:T(4,128)(2,1)} %param.16) | data formatting | bytes 327680 | tf_op jit(solution)/shard_map/reshape | solution.py:605
  2.3 94.1 %learn.1 = (bf16[512,5120]{1,0:T(8,128)(2,1)}, f32[320,1024]{1,0:T(8,128)}, f32[320,1024]{1,0:T(8,128)}, bf16[2,16,128]{2,1,0:T(8,128)(2,1)}, bf16[4,4,640]{2,1,0:T(4,128)(2,1)}) custom-call(bf16[512,5120]{1,0:T(8,128)(2,1)} %x_hbm.1, bf16[512,1024]{1,0:T(8,128)(2,1)} %u.1, f32[320,1024]{1,0:T(8,128)} %master_hbm.1, f32[320,1024]{1,0:T(8,128)} %m1_hbm.1, ...), custom_call_target="tpu_custom_call" | custom-call | flops 60000002048 | bytes 160000000 | tf_op jit(solution)/shard_map/learn/pallas_call | solution.py:569
  96.4 1.3 %copy.18 = bf16[2,4,4,128]{3,0,2,1:T(2,128)(2,1)} copy(bf16[2,4,4,128]{3,2,1,0:T(4,128)(2,1)} %bitcast.5) | data formatting | bytes 16384 | tf_op jit(solution)/shard_map/reshape | solution.py:620
  97.7 0.0 copy-start.1
  97.7 5.3 %copy.23 = bf16[512,5120]{1,0:T(8,128)(2,1)} copy(bf16[512,5120]{1,0:T(8,128)(2,1)} %get-tuple-element.20) | data formatting | bytes 10485760
  103.0 0.0 copy-done.1
  103.0 0.0 copy-start
  103.0 1.1 copy.24
  104.0 0.7 copy-done
  104.8 0.0 copy-start.2
  104.8 1.1 copy.25
  105.8 0.0 copy-done.2
  105.8 0.6 copy.26
Async XLA Ops:
  97.7 5.3 %copy-start.1 = (f32[320,1024]{1,0:T(8,128)S(1)}, f32[320,1024]{1,0:T(8,128)}, u32[]{:S(2)}) copy-start(f32[320,1024]{1,0:T(8,128)} %get-tuple-element.21) | copy-start | bytes 3932164
  103.0 1.8 %copy-start = (f32[320,1024]{1,0:T(8,128)S(1)}, f32[320,1024]{1,0:T(8,128)}, u32[]{:S(2)}) copy-start(f32[320,1024]{1,0:T(8,128)} %get-tuple-element.22) | copy-start | bytes 3932164
  104.8 1.1 copy-start.2

commit v3 on v2

v3 whole, which is shorter than its diff:
```python
import functools
import math

import jax
import jax.numpy as jnp
from jax import lax
from jax.experimental import pallas as pl
from jax.experimental.pallas import tpu as pltpu
from jax.sharding import PartitionSpec as P

HD = 128
GROUP = 5
MESH = pl.DeviceIdType.MESH


beta_one = 0.9
beta_two = 0.95
learn_rate = 0.004
decay_rate = 0.1
adam_eps = 1e-08
correction_one = 1.0 - 0.9**20
correction_two = 1.0 - 0.95**20

T1, D1, F1, C1, A2, C2, A3, C3 = 0, 8, 16, 24, 27, 39, 42, 45
XS, UT, GX, TP, HS, FR = 48, 52, 53, 54, 62, 78
WZ, WF, WY, WS, SEMS = 94, 96, 98, 106, 114
NT = (((1,), (1,)), ((), ()))

f32, bf16 = jnp.float32, jnp.bfloat16


def adamw(master, grad, moment_one, moment_two):
    new_first = beta_one * moment_one + (1.0 - beta_one) * grad
    new_second = beta_two * moment_two + (1.0 - beta_two) * grad * grad
    update = new_first / correction_one / (jnp.sqrt(new_second / correction_two) + adam_eps)
    return (master - learn_rate * (update + decay_rate * master), new_first)


def learn_kernel(
    grad_factor,
    x_hbm,
    u,
    master_hbm,
    m1_hbm,
    m2_hbm,
    hidden,
    kw_hbm,
    queries,
    k_hbm,
    v_hbm,
    lengths,
    wall,
    gall,
    fresh_out,
    attended,
    ut,
    wown,
    kw,
    keys,
    values,
    qf,
    acc,
    fprob,
    x_own,
    x_sib,
    ut_sib,
    master,
    m1,
    m2,
    ga,
    gc,
    t1,
    r1a,
    r1c,
    s1a,
    s1c,
    r2a,
    r2c,
    s2a,
    s2c,
    r3a,
    r3c,
    gx,
    gt,
    gown,
    wpad,
    hr,
    pf,
    fr,
    ssem,
    rsem,
    lsem,
):
    f, t = lax.axis_index("fsdp"), lax.axis_index("tp")
    z, yl, c = f // 4, (f // 2) % 2, f % 2
    yh, x = t // 4, t % 4
    y = yh * 2 + yl
    sib = (z * 4 + yl * 2 + (1 - c), t)
    own = z * 2 + yl

    def dev_x(d):
        return (f, yh * 4 + (x + d) % 4)

    def dev_y(d):
        yy = (y + d) % 4
        return (z * 4 + (yy % 2) * 2 + c, (yy // 2) * 4 + x)

    def dev_z(d):
        return (((z + d) % 4) * 4 + yl * 2 + c, t)

    def rcopy(src, dst, n, who):
        return pltpu.make_async_remote_copy(
            src_ref=src,
            dst_ref=dst,
            send_sem=ssem.at[n],
            recv_sem=rsem.at[n],
            device_id=who,
            device_id_type=MESH,
        )

    def lanes(zz):
        return pl.ds(pl.multiple_of(zz * 1280, 1280), 1280)

    tcols = pl.ds(pl.multiple_of(t * 128, 128), 128)
    local = [(master_hbm, master)]
    local += [(x_hbm.at[:, lanes((z + k) % 4)], x_own.at[:, lanes((z + k) % 4)]) for k in (1, 2, 3, 4)]
    local += [(kw_hbm, kw), (k_hbm, keys), (v_hbm, values)]
    local += [(m1_hbm.at[:, tcols], m1), (m2_hbm.at[:, tcols], m2)]
    local = [pltpu.make_async_copy(a, b, lsem.at[i]) for i, (a, b) in enumerate(local)]
    for cp in local:
        cp.start()
    own_out = pltpu.make_async_copy(wown, wall.at[own, c], lsem.at[10])
    grad_out = pltpu.make_async_copy(gown, gall.at[t], lsem.at[11])

    barrier = pltpu.get_barrier_semaphore()

    @pl.loop(1, 16)
    def _(j):
        pl.semaphore_signal(barrier, 1, device_id=((f + j) % 16, t), device_id_type=MESH)

    @pl.loop(1, 8)
    def _(j):
        pl.semaphore_signal(barrier, 1, device_id=(f, (t + j) % 8), device_id_type=MESH)

    pl.semaphore_signal(
        barrier,
        1,
        device_id=(z * 4 + (1 - yl) * 2 + c, (1 - yh) * 4 + x),
        device_id_type=MESH,
    )

    for tt in range(8):
        block = u[:, tt * 128 : (tt + 1) * 128].T
        place = ((tt % 4) * 2 + tt // 4) * 64
        ut[0, place : place + 64] = block[0:64]
        ut[1, place : place + 64] = block[64:128]
    local[0].wait()
    wown[...] = master[...].astype(bf16)
    own_out.start()
    pl.semaphore_wait(barrier, 23)

    ut_copy = rcopy(ut.at[1 - c], ut_sib, UT, sib)
    ut_copy.start()
    sib_copies = [
        rcopy(x_hbm.at[:, lanes((z + k) % 4)], x_sib.at[:, lanes((z + k) % 4)], XS + k - 1, sib)
        for k in (1, 2, 3, 4)
    ]
    for cp in sib_copies:
        cp.start()

    def wz(i):
        return rcopy(wown, wall.at[own, c], WZ + i, dev_z(1 if i == 0 else 3))

    def wf(i):
        rows = pl.ds(i * 160, 160)
        piece = wall.at[((z + (3 if i == 0 else 1)) % 4) * 2 + yl, c, rows]
        return rcopy(piece, piece, WF + i, dev_z(1 if i == 0 else 3))

    def wy(dz, way):
        rows = pl.ds(way * 160, 160)
        piece = wall.at[((z + dz) % 4) * 2 + yl, c, rows]
        source = wown.at[rows] if dz == 0 else piece
        return rcopy(source, piece, WY + dz * 2 + way, dev_y(1 if way == 0 else 3))

    def ws(dz, other):
        ll = 1 - yl if other else yl
        piece = wall.at[((z + dz) % 4) * 2 + ll, c]
        source = wown if (dz, other) == (0, 0) else piece
        return rcopy(source, piece, WS + other * 4 + dz, sib)

    for i in range(2):
        wz(i).start()
    for way in range(2):
        wy(0, way).start()

    def hidden_copy(j):
        to = (f + j) % 16
        cols = pl.ds(pl.multiple_of((to // 2) * 640, 640), 640)
        return rcopy(hidden.at[:, cols], hr.at[j], HS + j, (to, t))

    @pl.loop(1, 16)
    def _(j):
        hidden_copy(j).start()

    hr[0] = hidden[:, pl.ds(pl.multiple_of((f // 2) * 640, 640), 640)]
    wpad[...] = jnp.zeros_like(wpad)

    right, left = (x + 1) % 4, (x + 3) % 4

    def two_hop(i, zz, k):
        return rcopy(
            ga.at[(x + 2) % 4, i, zz], t1.at[i, zz], T1 + i * 4 + k, dev_x(1 if i == 0 else 3)
        )

    def direct(i, zz, k):
        piece = ga.at[right if i == 0 else left, 1 - i, zz]
        return rcopy(piece, r1a.at[i, 1 - i, zz], D1 + i * 4 + k, dev_x(1 if i == 0 else 3))

    def summed(i, zz, k):
        piece = ga.at[right if i == 0 else left, i, zz]
        return rcopy(piece, r1a.at[i, i, zz], F1 + i * 4 + k, dev_x(1 if i == 0 else 3))

    def c1(d):
        return rcopy(gc.at[:, :, (z + d) % 4], r1c.at[d - 1], C1 + d - 1, dev_z(d))

    def a2(d, zz, k):
        yy = (y + d) % 4
        return rcopy(
            s1a.at[yy // 2, zz, yy % 2], r2a.at[d - 1, zz], A2 + (d - 1) * 4 + k, dev_y(d)
        )

    def c2(d):
        return rcopy(s1c.at[(x + d) % 4], r2c.at[d - 1], C2 + d - 1, dev_x(d))

    def a3(d):
        return rcopy(s2a.at[(z + d) % 4], r3a.at[d - 1], A3 + d - 1, dev_z(d))

    def c3(d):
        yy = (y + d) % 4
        return rcopy(s2c.at[yy // 2, yy % 2], r3c.at[d - 1], C3 + d - 1, dev_y(d))

    def pass_on(k):
        zz = (z + 1 + k) % 4
        for i in range(2):
            two_hop(i, zz, k).wait()
            to = right if i == 0 else left

            @pl.loop(0, 2)
            def _(ll):
                got = ga[to, i, zz, ll].astype(f32) + t1[i, zz, ll].astype(f32)
                ga[to, i, zz, ll] = got.astype(bf16)

            summed(i, zz, k).start()

    ut_copy.wait()
    for k in range(4):
        zz = (z + 1 + k) % 4
        local[1 + k].wait()
        sib_copies[k].wait()

        @pl.loop(0, 4)
        def _(i):
            ll, half = i // 2, i % 2
            cols = pl.ds(pl.multiple_of(zz * 1280 + ll * 640, 640), 640)
            rows = pl.ds(pl.multiple_of(half * 256, 256), 256)
            part = jnp.dot(ut[c, rows], x_own[:, cols], preferred_element_type=f32)
            part += jnp.dot(ut_sib[rows], x_sib[:, cols], preferred_element_type=f32)
            part = part.astype(bf16)
            for b in range(4):
                xx, hh = half * 2 + b // 2, b % 2
                ga[xx, hh, zz, ll] = part[b * 64 : (b + 1) * 64, 0:512]
                gc[xx, hh, zz, ll] = part[b * 64 : (b + 1) * 64, 512:640]

        for i in range(2):
            two_hop(i, zz, k).start()
        for i in range(2):
            direct(i, zz, k).start()
        if k < 3:
            c1(k + 1).start()
        if k > 0:
            pass_on(k - 1)
    pass_on(3)
    ws(0, 0).start()

    for i in range(2):
        wz(i).wait()
    for i in range(2):
        wf(i).start()
    for dz in (1, 3):
        for way in range(2):
            wy(dz, way).start()
        ws(dz, 0).start()

    local[5].wait()
    fresh_out[0] = jnp.dot(hidden[...], kw[...], preferred_element_type=f32).astype(bf16)
    qf[...] = jnp.zeros_like(qf)
    for step in range(4):
        for g in range(GROUP):
            qf[:, step * GROUP + g] = queries[step, :, g * HD : (g + 1) * HD].astype(f32)
    local[6].wait()
    local[7].wait()
    scale = 1.0 / math.sqrt(HD)

    def attend(r):
        q = qf[r].astype(bf16)
        scores = lax.dot_general(q, keys[r], NT, preferred_element_type=f32) * scale
        slots = lax.broadcasted_iota(jnp.int32, (32, 4096), 1)
        scores = jnp.where(slots < lengths[r], scores, -1e30)
        extra = lax.dot_general(q, fresh_out[0], NT, preferred_element_type=f32) * scale
        line = lax.broadcasted_iota(jnp.int32, (32, 16), 0)
        item = lax.broadcasted_iota(jnp.int32, (32, 16), 1)
        seen = ((item & 3) == r) & ((item >> 2) * GROUP <= line)
        extra = jnp.where(seen, extra, -1e30)
        highest = jnp.maximum(
            jnp.max(scores, axis=1, keepdims=True), jnp.max(extra, axis=1, keepdims=True)
        )
        scores = jnp.exp(scores - highest)
        extra = jnp.exp(extra - highest)
        norm = 1.0 / (
            jnp.sum(scores, axis=1, keepdims=True) + jnp.sum(extra, axis=1, keepdims=True)
        )
        fprob[r] = (extra * norm).astype(bf16)
        acc[r] = jnp.dot((scores * norm).astype(bf16), values[r], preferred_element_type=f32)

    def total(own, others, index, count=3):
        got = own.astype(f32)
        for d in range(count):
            got += others[(d,) + index].astype(f32)
        return got

    for k in range(4):
        zz = (z + 1 + k) % 4
        for i in range(2):
            direct(i, zz, k).wait()
            summed(i, zz, k).wait()

        @pl.loop(0, 4)
        def _(i):
            hh, ll = i // 2, i % 2
            s1a[hh, zz, ll] = total(ga[x, hh, zz, ll], r1a, (hh, zz, ll), 2).astype(bf16)

        for d in (2, 1, 3):
            a2(d, zz, k).start()

        @pl.loop(k, k + 1)
        def _(r):
            attend(r)

    for i in range(2):
        wf(i).wait()
    for way in range(2):
        wy(2, way).start()
    ws(2, 0).start()
    for d in (1, 2, 3):
        c1(d).wait()

    @pl.loop(0, 16)
    def _(i):
        xx, hh, ll = i // 4, (i // 2) % 2, i % 2
        s1c[xx, hh, ll] = total(gc[xx, hh, z, ll], r1c, (xx, hh, ll)).astype(bf16)

    for d in (2, 1, 3):
        c2(d).start()

    for k in range(4):
        zz = (z + 1 + k) % 4
        for d in (1, 2, 3):
            a2(d, zz, k).wait()
        s2a[zz] = total(s1a[yh, zz, yl], r2a, (zz,))
        if k < 3:
            a3(k + 1).start()
    for d in (1, 2, 3):
        c2(d).wait()

    @pl.loop(0, 4)
    def _(i):
        hh, ll = i // 2, i % 2
        s2c[hh, ll] = total(s1c[x, hh, ll], r2c, (hh, ll))

    for d in (2, 1, 3):
        c3(d).start()

    for d in (1, 2, 3):
        a3(d).wait()
        c3(d).wait()
    gx[c, :, 0:512] = total(s2a[z], r3a, ()) * grad_factor
    gx[c, :, 512:640] = total(s2c[yh, yl], r3c, ()) * grad_factor
    gx_copy = rcopy(gx.at[c], gx.at[c], GX, sib)
    gx_copy.start()
    gx_copy.wait()
    gt[...] = gx[...].reshape(128, 640).T
    mine = pl.ds(pl.multiple_of(c * 320, 320), 320)
    gown[...] = gt[mine, :].astype(bf16)
    grad_out.start()

    def tp_copy(j):
        return rcopy(gown, gall.at[t], TP + j, (f, (t + j) % 8))

    @pl.loop(1, 8)
    def _(j):
        tp_copy(j).start()

    local[8].wait()
    local[9].wait()
    stepped, _ = adamw(master[:, tcols], gown[...].astype(f32), m1[...], m2[...])
    wpad[mine, :] = stepped.astype(bf16)

    @pl.loop(1, 16)
    def _(j):
        hidden_copy(j).wait()

    pf[...] = jnp.dot(
        hr[...].reshape(256, 640), wpad[...], preferred_element_type=f32
    ).reshape(16, 16, 128)

    def fresh_copy(j):
        return rcopy(pf.at[j], fr.at[j], FR + j, ((f + 16 - j) % 16, t))

    @pl.loop(1, 16)
    def _(j):
        fresh_copy(j).start()

    for dz in (0, 1, 3, 2):
        for way in range(2):
            wy(dz, way).wait()
        ws(dz, 1).start()

    @pl.loop(1, 16)
    def _(j):
        fresh_copy(j).wait()

    fr[0] = pf[0]
    fresh_out[1] = jnp.sum(fr[...], axis=0).astype(bf16)

    @pl.loop(0, 4)
    def _(r):
        acc[r] += jnp.dot(fprob[r], fresh_out[1], preferred_element_type=f32)

    for step in range(4):
        for g in range(GROUP):
            attended[step, :, g * HD : (g + 1) * HD] = acc[:, step * GROUP + g].astype(bf16)

    own_out.wait()
    grad_out.wait()

    @pl.loop(1, 8)
    def _(j):
        tp_copy(j).wait()

    for other in range(2):
        for dz in range(4):
            ws(dz, other).wait()


def learn(
    inputs, upstream, master, m1, m2, flat, key_weight, queries, keys, values, lengths, grad_factor
):
    hbm = pl.BlockSpec(memory_space=pl.ANY)
    vmem = pl.BlockSpec(memory_space=pltpu.VMEM)
    smem = pl.BlockSpec(memory_space=pltpu.SMEM)
    shape = jax.ShapeDtypeStruct
    V = pltpu.VMEM
    scratch = [
        V((2, 512, 512), bf16),
        V((320, 1024), bf16),
        V((5120, 128), bf16),
        V((4, 4096, 128), bf16),
        V((4, 4096, 128), bf16),
        V((4, 32, 128), f32),
        V((4, 32, 128), f32),
        V((4, 32, 16), bf16),
        V((512, 5120), bf16),
        V((512, 5120), bf16),
        V((512, 512), bf16),
        V((320, 1024), f32),
        V((320, 128), f32),
        V((320, 128), f32),
        V((4, 2, 4, 2, 64, 512), bf16),
        V((4, 2, 4, 2, 64, 128), bf16),
        V((2, 4, 2, 64, 512), bf16),
        V((2, 2, 4, 2, 64, 512), bf16),
        V((3, 4, 2, 2, 64, 128), bf16),
        V((2, 4, 2, 64, 512), bf16),
        V((4, 2, 2, 64, 128), bf16),
        V((3, 4, 64, 512), bf16),
        V((3, 2, 2, 64, 128), bf16),
        V((4, 64, 512), f32),
        V((2, 2, 64, 128), f32),
        V((3, 64, 512), f32),
        V((3, 64, 128), f32),
        V((2, 64, 640), f32),
        V((640, 128), f32),
        V((320, 128), bf16),
        V((640, 128), bf16),
        V((16, 16, 640), bf16),
        V((16, 16, 128), f32),
        V((16, 16, 128), f32),
        pltpu.SemaphoreType.DMA((SEMS,)),
        pltpu.SemaphoreType.DMA((SEMS,)),
        pltpu.SemaphoreType.DMA((12,)),
    ]
    return pl.pallas_call(
        functools.partial(learn_kernel, grad_factor),
        out_shape=(
            shape((8, 2, 320, 1024), bf16),
            shape((8, 320, 128), bf16),
            shape((2, 16, 128), bf16),
            shape((4, 4, 640), bf16),
        ),
        in_specs=[hbm, vmem, hbm, hbm, hbm, vmem, hbm, vmem, hbm, hbm, smem],
        out_specs=[hbm, hbm, vmem, vmem],
        scratch_shapes=scratch,
        name="learn",
        compiler_params=pltpu.CompilerParams(
            collective_id=0, has_side_effects=True, vmem_limit_bytes=56 << 20
        ),
    )(inputs, upstream, master, m1, m2, flat, key_weight, queries, keys, values, lengths)


def finish_kernel(u, w, grad, master, m1, m2, input_grad, new_master, new_moment):
    input_grad[...] = lax.dot_general(u[...], w[...], NT, preferred_element_type=f32).astype(bf16)
    new_master[...], new_moment[...] = adamw(
        master[...], grad[...].astype(f32), m1[...], m2[...]
    )


def finish(upstream, weight, grad, master, m1, m2):
    cols = pl.BlockSpec((320, 128), lambda i: (0, i))
    return pl.pallas_call(
        finish_kernel,
        grid=(8,),
        out_shape=(
            jax.ShapeDtypeStruct((512, 5120), bf16),
            jax.ShapeDtypeStruct((320, 1024), f32),
            jax.ShapeDtypeStruct((320, 1024), f32),
        ),
        in_specs=[
            pl.BlockSpec((512, 1024), lambda i: (0, 0)),
            pl.BlockSpec((640, 1024), lambda i: (i, 0)),
            pl.BlockSpec((None, 320, 128), lambda i: (i, 0, 0)),
            cols,
            cols,
            cols,
        ],
        out_specs=[pl.BlockSpec((512, 640), lambda i: (0, i)), cols, cols],
        name="finish",
        compiler_params=pltpu.CompilerParams(vmem_limit_bytes=32 << 20),
    )(upstream, weight, grad, master, m1, m2)


def shards(
    inputs,
    upstream,
    master,
    moment_one,
    moment_two,
    hidden_steps,
    key_weight,
    queries,
    key_cache,
    value_cache,
    lengths,
):
    grad_factor = 1.0 / math.sqrt(inputs.shape[0] * lax.axis_size("fsdp") * lax.axis_size("tp"))
    flat = hidden_steps.reshape(16, 5120)
    weight, grad, fresh, attended = learn(
        inputs,
        upstream,
        master,
        moment_one,
        moment_two,
        flat,
        key_weight,
        queries,
        key_cache,
        value_cache,
        lengths,
        grad_factor,
    )
    input_grad, new_master, new_moment = finish(
        upstream, weight.reshape(5120, 1024), grad, master, moment_one, moment_two
    )
    fresh_kv = fresh.reshape(2, 4, 4, 128).transpose(1, 2, 0, 3)
    return (input_grad, new_master, new_moment, fresh_kv, attended)


def solution(mesh):
    in_specs = (
        P(("fsdp", "tp"), None),
        P(("fsdp", "tp"), None),
        P("fsdp", None),
        P("fsdp", None),
        P("fsdp", None),
        P(None, "fsdp", None),
        P(None, "tp"),
        P(None, "fsdp", "tp"),
        P("fsdp", None, "tp"),
        P("fsdp", None, "tp"),
        P("fsdp"),
    )
    out_specs = (
        P(("fsdp", "tp"), None),
        P("fsdp", None),
        P("fsdp", None),
        P(None, "fsdp", None, "tp"),
        P(None, "fsdp", "tp"),
    )
    return jax.shard_map(shards, mesh=mesh, in_specs=in_specs, out_specs=out_specs, check_vma=False)
```

time: 107 us -> 116 us (1.084)
  Pallas kernels: 94.1 us -> 108 us
  local copies, waits for them, and re-layouts: 11.7 us -> 7.92 us
    pallas_call x0 -> x1, Pallas kernels: none -> 10.9 us  [finish(): pl.pallas_call(finish_kernel, grid=(8,), out_shape=(jax.ShapeDtypeStruct(...]
    unnamed x10 -> x17, local copies, waits for them, and re-layouts: 8.74 us -> 5.69 us
    pallas_call x1, Pallas kernels: 94.1 us -> 96.7 us  [learn(): pl.pallas_call(functools.partial(learn_kernel, grad_factor), out_shape=(s...]
where the time goes in v3:
time: 116 us
  Pallas kernels  108 us (93%)
  local copies, waits for them, and re-layouts  7.92 us (7%)
    pallas_call x1, Pallas kernels, learn(): pl.pallas_call(functools.partial(learn_kernel, grad_factor), out_shape=(s...  96.7 us
    pallas_call x1, Pallas kernels, finish(): pl.pallas_call(finish_kernel, grid=(8,), out_shape=(jax.ShapeDtypeStruct(...  10.9 us
    unnamed x17, local copies, waits for them, and re-layouts  5.69 us

profile of v3, /device:TPU:1, one launch (start us, length us, event | category | flops | bytes accessed | tf_op | source)
XLA Modules:
  0.0 116.2 jit_solution(5332359691401838341)
XLA Ops:
  0.6 1.6 %reshape.19.hidden = bf16[16,5120]{1,0:T(8,128)(2,1)} reshape(bf16[4,4,5120]{2,1,0:T(4,128)(2,1)} %param.16) | data formatting | bytes 327680 | tf_op jit(solution)/shard_map/reshape | solution.py:565
  2.3 0.0 copy-start.1
  2.3 0.0 copy-start.2
  2.3 0.0 copy-start.3
  2.3 0.0 copy-start.4
  2.3 96.7 %learn.1 = (bf16[8,2,320,1024]{3,2,1,0:T(8,128)(2,1)}, bf16[8,320,128]{2,1,0:T(8,128)(2,1)}, bf16[2,16,128]{2,1,0:T(8,128)(2,1)}, bf16[4,4,640]{2,1,0:T(4,128)(2,1)}) custom-call(bf16[512,5120]{1,0:T(8,128)(2,1)} %x_hbm.1, bf16[512,1024]{1,0:T(8,128)(2,1)} %u.3, f32[320,1024]{1,0:T(8,128)} %master.1, f32[320,1024]{1,0:T(8,128)} %m1.1, f32[320,1024]{1,0:T(8,128)} %m2.1, ...), custom_call_target="tpu_custom_call" | custom-call | tf_op jit(solution)/shard_map/learn/pallas_call | solution.py:502
  99.0 0.0 copy-done.1
  99.0 0.0 copy-done.2
  99.0 0.0 copy-done.3
  99.0 0.0 copy-done.4
  99.0 0.0 copy-start
  99.1 4.0 %copy-done = bf16[8,2,320,1024]{3,2,1,0:T(8,128)(2,1)S(1)} copy-done((bf16[8,2,320,1024]{3,2,1,0:T(8,128)(2,1)S(1)}, bf16[8,2,320,1024]{3,2,1,0:T(8,128)(2,1)}, u32[]{:S(2)}) %copy-start) | copy-done | bytes 10485784
  103.0 0.0 copy-start.5
  103.0 1.1 copy-done.5
  104.1 0.0 copy-start.7
  104.1 0.0 copy-start.6
  104.1 10.9 %finish.1 = (bf16[512,5120]{1,0:T(8,128)(2,1)}, f32[320,1024]{1,0:T(8,128)}, f32[320,1024]{1,0:T(8,128)}) custom-call(bf16[512,1024]{1,0:T(8,128)(2,1)S(1)} %copy-done.4, bf16[5120,1024]{1,0:T(8,128)(2,1)S(1)} %bitcast.5, bf16[8,320,128]{2,1,0:T(8,128)(2,1)S(1)} %copy-done.5, f32[320,1024]{1,0:T(8,128)S(1)} %copy-done.1, f32[320,1024]{1,0:T(8,128)S(1)} %copy-done.2, ...), custom_call_target="tpu_custom_call" | custom-call | tf_op jit(solution)/shard_map/finish/pallas_call | solution.py:529
  115.0 0.0 copy-done.7
  115.0 0.6 copy.18
  115.6 0.0 copy-done.6
  115.6 0.6 copy.20
Async XLA Ops:
  2.3 96.8 %copy-start.1 = (f32[320,1024]{1,0:T(8,128)S(1)}, f32[320,1024]{1,0:T(8,128)}, u32[]{:S(2)}) copy-start(f32[320,1024]{1,0:T(8,128)} %master.1) | copy-start | bytes 3932164
  2.3 96.8 %copy-start.2 = (f32[320,1024]{1,0:T(8,128)S(1)}, f32[320,1024]{1,0:T(8,128)}, u32[]{:S(2)}) copy-start(f32[320,1024]{1,0:T(8,128)} %m1.1) | copy-start | bytes 3932164
  2.3 96.8 %copy-start.3 = (f32[320,1024]{1,0:T(8,128)S(1)}, f32[320,1024]{1,0:T(8,128)}, u32[]{:S(2)}) copy-start(f32[320,1024]{1,0:T(8,128)} %m2.1) | copy-start | bytes 3932164
  2.3 96.8 %copy-start.4 = (bf16[512,1024]{1,0:T(8,128)(2,1)S(1)}, bf16[512,1024]{1,0:T(8,128)(2,1)}, u32[]{:S(2)}) copy-start(bf16[512,1024]{1,0:T(8,128)(2,1)} %u.3) | copy-start | bytes 3145732
  99.0 4.0 %copy-start = (bf16[8,2,320,1024]{3,2,1,0:T(8,128)(2,1)S(1)}, bf16[8,2,320,1024]{3,2,1,0:T(8,128)(2,1)}, u32[]{:S(2)}) copy-start(bf16[8,2,320,1024]{3,2,1,0:T(8,128)(2,1)} %get-tuple-element.12) | copy-start | bytes 31457284
  103.0 1.1 copy-start.5
  104.1 10.9 %copy-start.7 = (bf16[2,16,128]{2,1,0:T(8,128)(2,1)S(1)}, bf16[2,16,128]{2,1,0:T(8,128)(2,1)}, u32[]{:S(2)}) copy-start(bf16[2,16,128]{2,1,0:T(8,128)(2,1)} %get-tuple-element.17) | copy-start | bytes 24580
  104.1 11.5 %copy-start.6 = (bf16[4,4,640]{2,1,0:T(4,128)(2,1)S(1)}, bf16[4,4,640]{2,1,0:T(4,128)(2,1)}, u32[]{:S(2)}) copy-start(bf16[4,4,640]{2,1,0:T(4,128)(2,1)} %get-tuple-element.28) | copy-start | bytes 61444

commit v4 on v3

--- a/solution.py
+++ b/solution.py
@@ -49,12 +49,13 @@
     k_hbm,
     v_hbm,
     lengths,
-    wall,
+    wother,
     gall,
+    part_hbm,
     fresh_out,
     attended,
     ut,
-    wown,
+    wsame,
     kw,
     keys,
     values,
@@ -96,7 +97,6 @@
     yh, x = t // 4, t % 4
     y = yh * 2 + yl
     sib = (z * 4 + yl * 2 + (1 - c), t)
-    own = z * 2 + yl
 
     def dev_x(d):
         return (f, yh * 4 + (x + d) % 4)
@@ -127,10 +127,9 @@
     local += [(kw_hbm, kw), (k_hbm, keys), (v_hbm, values)]
     local += [(m1_hbm.at[:, tcols], m1), (m2_hbm.at[:, tcols], m2)]
     local = [pltpu.make_async_copy(a, b, lsem.at[i]) for i, (a, b) in enumerate(local)]
-    for cp in local:
+    for cp in local[:5]:
         cp.start()
-    own_out = pltpu.make_async_copy(wown, wall.at[own, c], lsem.at[10])
-    grad_out = pltpu.make_async_copy(gown, gall.at[t], lsem.at[11])
+    grad_out = pltpu.make_async_copy(gown, gall.at[t], lsem.at[10])
 
     barrier = pltpu.get_barrier_semaphore()
 
@@ -155,8 +154,7 @@
         ut[0, place : place + 64] = block[0:64]
         ut[1, place : place + 64] = block[64:128]
     local[0].wait()
-    wown[...] = master[...].astype(bf16)
-    own_out.start()
+    wsame[z, c] = master[...].astype(bf16)
     pl.semaphore_wait(barrier, 23)
 
     ut_copy = rcopy(ut.at[1 - c], ut_sib, UT, sib)
@@ -165,28 +163,48 @@
         rcopy(x_hbm.at[:, lanes((z + k) % 4)], x_sib.at[:, lanes((z + k) % 4)], XS + k - 1, sib)
         for k in (1, 2, 3, 4)
     ]
-    for cp in sib_copies:
+    for cp in sib_copies[:2]:
         cp.start()
 
     def wz(i):
-        return rcopy(wown, wall.at[own, c], WZ + i, dev_z(1 if i == 0 else 3))
+        piece = wsame.at[z, c]
+        return rcopy(piece, piece, WZ + i, dev_z(1 if i == 0 else 3))
 
     def wf(i):
-        rows = pl.ds(i * 160, 160)
-        piece = wall.at[((z + (3 if i == 0 else 1)) % 4) * 2 + yl, c, rows]
+        piece = wsame.at[(z + (3 if i == 0 else 1)) % 4, c, pl.ds(i * 160, 160)]
         return rcopy(piece, piece, WF + i, dev_z(1 if i == 0 else 3))
 
     def wy(dz, way):
-        rows = pl.ds(way * 160, 160)
-        piece = wall.at[((z + dz) % 4) * 2 + yl, c, rows]
-        source = wown.at[rows] if dz == 0 else piece
-        return rcopy(source, piece, WY + dz * 2 + way, dev_y(1 if way == 0 else 3))
+        zz, rows = (z + dz) % 4, pl.ds(way * 160, 160)
+        return rcopy(
+            wsame.at[zz, c, rows],
+            wother.at[zz, c, rows],
+            WY + dz * 2 + way,
+            dev_y(1 if way == 0 else 3),
+        )
 
     def ws(dz, other):
-        ll = 1 - yl if other else yl
-        piece = wall.at[((z + dz) % 4) * 2 + ll, c]
-        source = wown if (dz, other) == (0, 0) else piece
-        return rcopy(source, piece, WS + other * 4 + dz, sib)
+        piece = (wother if other else wsame).at[(z + dz) % 4, c]
+        return rcopy(piece, piece, WS + other * 4 + dz, sib)
+
+    def part_out(dz):
+        zz = (z + dz) % 4
+        cols = pl.ds(pl.multiple_of(zz * 640, 640), 640)
+        return pltpu.make_async_copy(x_own.at[:, cols], part_hbm.at[zz], lsem.at[11 + dz])
+
+    def input_grad(dz):
+        ws(dz, 0).wait()
+
+        @pl.loop(0, 2)
+        def _(half):
+            zz = (z + dz) % 4
+            cols = pl.ds(pl.multiple_of(zz * 640, 640), 640)
+            rows = pl.ds(pl.multiple_of(half * 256, 256), 256)
+            x_own[rows, cols] = lax.dot_general(
+                u[rows], wsame[zz].reshape(640, 1024), NT, preferred_element_type=f32
+            ).astype(bf16)
+
+        part_out(dz).start()
 
     for i in range(2):
         wz(i).start()
@@ -257,6 +275,8 @@
         zz = (z + 1 + k) % 4
         local[1 + k].wait()
         sib_copies[k].wait()
+        if k < 2:
+            sib_copies[k + 2].start()
 
         @pl.loop(0, 4)
         def _(i):
@@ -279,8 +299,11 @@
             c1(k + 1).start()
         if k > 0:
             pass_on(k - 1)
+        if k == 1:
+            for cp in local[5:]:
+                cp.start()
+            ws(0, 0).start()
     pass_on(3)
-    ws(0, 0).start()
 
     for i in range(2):
         wz(i).wait()
@@ -328,7 +351,7 @@
             got += others[(d,) + index].astype(f32)
         return got
 
-    for k in range(4):
+    def first(k):
         zz = (z + 1 + k) % 4
         for i in range(2):
             direct(i, zz, k).wait()
@@ -342,33 +365,37 @@
         for d in (2, 1, 3):
             a2(d, zz, k).start()
 
-        @pl.loop(k, k + 1)
-        def _(r):
-            attend(r)
-
-    for i in range(2):
-        wf(i).wait()
-    for way in range(2):
-        wy(2, way).start()
-    ws(2, 0).start()
-    for d in (1, 2, 3):
-        c1(d).wait()
-
-    @pl.loop(0, 16)
-    def _(i):
-        xx, hh, ll = i // 4, (i // 2) % 2, i % 2
-        s1c[xx, hh, ll] = total(gc[xx, hh, z, ll], r1c, (xx, hh, ll)).astype(bf16)
-
-    for d in (2, 1, 3):
-        c2(d).start()
-
-    for k in range(4):
+    def second(k):
         zz = (z + 1 + k) % 4
         for d in (1, 2, 3):
             a2(d, zz, k).wait()
         s2a[zz] = total(s1a[yh, zz, yl], r2a, (zz,))
         if k < 3:
             a3(k + 1).start()
+
+    first(0)
+    pl.loop(0, 2)(attend)
+    for d in (1, 2, 3):
+        c1(d).wait()
+
+    @pl.loop(0, 16)
+    def _(i):
+        xx, hh, ll = i // 4, (i // 2) % 2, i % 2
+        s1c[xx, hh, ll] = total(gc[xx, hh, z, ll], r1c, (xx, hh, ll)).astype(bf16)
+
+    for d in (2, 1, 3):
+        c2(d).start()
+    first(1)
+    pl.loop(2, 4)(attend)
+    for i in range(2):
+        wf(i).wait()
+    for way in range(2):
+        wy(2, way).start()
+    ws(2, 0).start()
+    second(0)
+    first(2)
+    input_grad(0)
+    second(1)
     for d in (1, 2, 3):
         c2(d).wait()
 
@@ -379,6 +406,13 @@
 
     for d in (2, 1, 3):
         c3(d).start()
+    for way in range(2):
+        wy(0, way).wait()
+    ws(0, 1).start()
+    first(3)
+    second(2)
+    input_grad(1)
+    second(3)
 
     for d in (1, 2, 3):
         a3(d).wait()
@@ -420,10 +454,12 @@
     def _(j):
         fresh_copy(j).start()
 
-    for dz in (0, 1, 3, 2):
+    for dz in (1, 3, 2):
         for way in range(2):
             wy(dz, way).wait()
         ws(dz, 1).start()
+    input_grad(3)
+    input_grad(2)
 
     @pl.loop(1, 16)
     def _(j):
@@ -440,16 +476,15 @@
         for g in range(GROUP):
             attended[step, :, g * HD : (g + 1) * HD] = acc[:, step * GROUP + g].astype(bf16)
 
-    own_out.wait()
     grad_out.wait()
 
     @pl.loop(1, 8)
     def _(j):
         tp_copy(j).wait()
 
-    for other in range(2):
-        for dz in range(4):
-            ws(dz, other).wait()
+    for dz in range(4):
+        ws(dz, 1).wait()
+        part_out(dz).wait()
 
 
 def learn(
@@ -462,7 +497,7 @@
     V = pltpu.VMEM
     scratch = [
         V((2, 512, 512), bf16),
-        V((320, 1024), bf16),
+        V((4, 2, 320, 1024), bf16),
         V((5120, 128), bf16),
         V((4, 4096, 128), bf16),
         V((4, 4096, 128), bf16),
@@ -497,18 +532,19 @@
         V((16, 16, 128), f32),
         pltpu.SemaphoreType.DMA((SEMS,)),
         pltpu.SemaphoreType.DMA((SEMS,)),
-        pltpu.SemaphoreType.DMA((12,)),
+        pltpu.SemaphoreType.DMA((15,)),
     ]
     return pl.pallas_call(
         functools.partial(learn_kernel, grad_factor),
         out_shape=(
-            shape((8, 2, 320, 1024), bf16),
+            shape((4, 2, 320, 1024), bf16),
             shape((8, 320, 128), bf16),
+            shape((4, 512, 640), bf16),
             shape((2, 16, 128), bf16),
             shape((4, 4, 640), bf16),
         ),
         in_specs=[hbm, vmem, hbm, hbm, hbm, vmem, hbm, vmem, hbm, hbm, smem],
-        out_specs=[hbm, hbm, vmem, vmem],
+        out_specs=[hbm, hbm, hbm, vmem, vmem],
         scratch_shapes=scratch,
         name="learn",
         compiler_params=pltpu.CompilerParams(
@@ -517,18 +553,26 @@
     )(inputs, upstream, master, m1, m2, flat, key_weight, queries, keys, values, lengths)
 
 
-def finish_kernel(u, w, grad, master, m1, m2, input_grad, new_master, new_moment):
-    input_grad[...] = lax.dot_general(u[...], w[...], NT, preferred_element_type=f32).astype(bf16)
-    new_master[...], new_moment[...] = adamw(
-        master[...], grad[...].astype(f32), m1[...], m2[...]
-    )
-
-
-def finish(upstream, weight, grad, master, m1, m2):
-    cols = pl.BlockSpec((320, 128), lambda i: (0, i))
+def finish_kernel(u, part, w, grad, master, m1, m2, input_grad, new_master, new_moment):
+    yl = (lax.axis_index("fsdp") // 2) % 2
+    same = pl.ds(pl.multiple_of(yl * 640, 640), 640)
+    other = pl.ds(pl.multiple_of((1 - yl) * 640, 640), 640)
+    input_grad[:, same] = part[...]
+    input_grad[:, other] = lax.dot_general(
+        u[...], w[...], NT, preferred_element_type=f32
+    ).astype(bf16)
+    for i in range(2):
+        cols = slice(i * 128, (i + 1) * 128)
+        new_master[:, cols], new_moment[:, cols] = adamw(
+            master[:, cols], grad[i].astype(f32), m1[:, cols], m2[:, cols]
+        )
+
+
+def finish(upstream, part, weight, grad, master, m1, m2):
+    cols = pl.BlockSpec((320, 256), lambda i: (0, i))
     return pl.pallas_call(
         finish_kernel,
-        grid=(8,),
+        grid=(4,),
         out_shape=(
             jax.ShapeDtypeStruct((512, 5120), bf16),
             jax.ShapeDtypeStruct((320, 1024), f32),
@@ -536,16 +580,17 @@
         ),
         in_specs=[
             pl.BlockSpec((512, 1024), lambda i: (0, 0)),
+            pl.BlockSpec((None, 512, 640), lambda i: (i, 0, 0)),
             pl.BlockSpec((640, 1024), lambda i: (i, 0)),
-            pl.BlockSpec((None, 320, 128), lambda i: (i, 0, 0)),
+            pl.BlockSpec((2, 320, 128), lambda i: (i, 0, 0)),
             cols,
             cols,
             cols,
         ],
-        out_specs=[pl.BlockSpec((512, 640), lambda i: (0, i)), cols, cols],
+        out_specs=[pl.BlockSpec((512, 1280), lambda i: (0, i)), cols, cols],
         name="finish",
-        compiler_params=pltpu.CompilerParams(vmem_limit_bytes=32 << 20),
-    )(upstream, weight, grad, master, m1, m2)
+        compiler_params=pltpu.CompilerParams(vmem_limit_bytes=60 << 20),
+    )(upstream, part, weight, grad, master, m1, m2)
 
 
 def shards(
@@ -563,7 +608,7 @@
 ):
     grad_factor = 1.0 / math.sqrt(inputs.shape[0] * lax.axis_size("fsdp") * lax.axis_size("tp"))
     flat = hidden_steps.reshape(16, 5120)
-    weight, grad, fresh, attended = learn(
+    weight, grad, part, fresh, attended = learn(
         inputs,
         upstream,
         master,
@@ -578,7 +623,7 @@
         grad_factor,
     )
     input_grad, new_master, new_moment = finish(
-        upstream, weight.reshape(5120, 1024), grad, master, moment_one, moment_two
+        upstream, part, weight.reshape(2560, 1024), grad, master, moment_one, moment_two
     )
     fresh_kv = fresh.reshape(2, 4, 4, 128).transpose(1, 2, 0, 3)
     return (input_grad, new_master, new_moment, fresh_kv, attended)

time: 116 us -> 113 us (0.974)
  local copies, waits for them, and re-layouts: 7.92 us -> 2.84 us
    unnamed x17 -> x5, local copies, waits for them, and re-layouts: 5.69 us -> 0.61 us
    pallas_call x1, Pallas kernels: 96.7 us -> 98.1 us  [learn(): pl.pallas_call(functools.partial(learn_kernel, grad_factor), out_shape=(s...]
where the time goes in v4:
time: 113 us
  Pallas kernels  109 us (96%)
  local copies, waits for them, and re-layouts  2.84 us (3%)
    pallas_call x1, Pallas kernels, learn(): pl.pallas_call(functools.partial(learn_kernel, grad_factor), out_shape=(s...  98.1 us
    pallas_call x1, Pallas kernels, finish(): pl.pallas_call(finish_kernel, grid=(4,), out_shape=(jax.ShapeDtypeStruct(...  11 us

profile of v4, /device:TPU:1, one launch (start us, length us, event | category | flops | bytes accessed | tf_op | source)
XLA Modules:
  0.0 112.6 jit_solution(13926849448301913933)
XLA Ops:
  0.6 1.6 %reshape.19.hidden = bf16[16,5120]{1,0:T(8,128)(2,1)} reshape(bf16[4,4,5120]{2,1,0:T(4,128)(2,1)} %param.16) | data formatting | bytes 327680 | tf_op jit(solution)/shard_map/reshape | solution.py:610
  2.3 98.1 %learn.1 = (bf16[4,2,320,1024]{3,2,1,0:T(8,128)(2,1)}, bf16[8,320,128]{2,1,0:T(8,128)(2,1)}, bf16[4,512,640]{2,1,0:T(8,128)(2,1)}, bf16[2,16,128]{2,1,0:T(8,128)(2,1)}, bf16[4,4,640]{2,1,0:T(4,128)(2,1)}) custom-call(bf16[512,5120]{1,0:T(8,128)(2,1)} %x_hbm.1, bf16[512,1024]{1,0:T(8,128)(2,1)} %u.3, f32[320,1024]{1,0:T(8,128)} %master.1, f32[320,1024]{1,0:T(8,128)} %m1.1, ...), custom_call_target="tpu_custom_call" | custom-call | tf_op jit(solution)/shard_map/learn/pallas_call | solution.py:537
  100.4 0.0 copy-start.1
  100.4 0.0 copy-start
  100.4 11.0 %finish.1 = (bf16[512,5120]{1,0:T(8,128)(2,1)}, f32[320,1024]{1,0:T(8,128)}, f32[320,1024]{1,0:T(8,128)}) custom-call(bf16[512,1024]{1,0:T(8,128)(2,1)} %u.3, bf16[4,512,640]{2,1,0:T(8,128)(2,1)} %get-tuple-element.13.part, bf16[2560,1024]{1,0:T(8,128)(2,1)} %bitcast.5, bf16[8,320,128]{2,1,0:T(8,128)(2,1)} %get-tuple-element.15.grad, f32[320,1024]{1,0:T(8,128)} %master.1, ...), custom_call_target="tpu_custom_call" | custom-call | tf_op jit(solution)/shard_map/finish/pallas_call | solution.py:573
  111.4 0.0 copy-done.1
  111.4 0.6 copy.18
  112.0 0.0 copy-done
  112.0 0.6 copy.20
Async XLA Ops:
  100.4 11.0 %copy-start.1 = (bf16[2,16,128]{2,1,0:T(8,128)(2,1)S(1)}, bf16[2,16,128]{2,1,0:T(8,128)(2,1)}, u32[]{:S(2)}) copy-start(bf16[2,16,128]{2,1,0:T(8,128)(2,1)} %get-tuple-element.19) | copy-start | bytes 24580
  100.4 11.6 %copy-start = (bf16[4,4,640]{2,1,0:T(4,128)(2,1)S(1)}, bf16[4,4,640]{2,1,0:T(4,128)(2,1)}, u32[]{:S(2)}) copy-start(bf16[4,4,640]{2,1,0:T(4,128)(2,1)} %get-tuple-element.30) | copy-start | bytes 61444

commit v5 on v4

--- a/solution.py
+++ b/solution.py
@@ -23,7 +23,8 @@
 
 T1, D1, F1, C1, A2, C2, A3, C3 = 0, 8, 16, 24, 27, 39, 42, 45
 XS, UT, GX, TP, HS, FR = 48, 52, 53, 54, 62, 78
-WZ, WF, WY, WS, SEMS = 94, 96, 98, 106, 114
+WZ, WF, WY, WS, WX, B1, B2, B3, SEMS = 94, 96, 98, 114, 122, 134, 146, 149, 152
+WHOLE, QUARTER = 192, 32
 NT = (((1,), (1,)), ((), ()))
 
 f32, bf16 = jnp.float32, jnp.bfloat16
@@ -69,17 +70,23 @@
     m1,
     m2,
     ga,
+    gb,
     gc,
     t1,
     r1a,
+    r1b,
     r1c,
     s1a,
+    s1b,
     s1c,
     r2a,
+    r2b,
     r2c,
     s2a,
+    s2b,
     s2c,
     r3a,
+    r3b,
     r3c,
     gx,
     gt,
@@ -166,6 +173,8 @@
     for cp in sib_copies[:2]:
         cp.start()
 
+    quarter = WHOLE + x * QUARTER
+
     def wz(i):
         piece = wsame.at[z, c]
         return rcopy(piece, piece, WZ + i, dev_z(1 if i == 0 else 3))
@@ -174,14 +183,37 @@
         piece = wsame.at[(z + (3 if i == 0 else 1)) % 4, c, pl.ds(i * 160, 160)]
         return rcopy(piece, piece, WF + i, dev_z(1 if i == 0 else 3))
 
-    def wy(dz, way):
-        zz, rows = (z + dz) % 4, pl.ds(way * 160, 160)
+    def wy(dz, way, part):
+        zz = (z + dz) % 4
+        first = (way * (WHOLE // 2), pl.multiple_of(quarter + way * (QUARTER // 2), 16))[part]
+        rows = pl.ds(first, (WHOLE // 2, QUARTER // 2)[part])
         return rcopy(
             wsame.at[zz, c, rows],
             wother.at[zz, c, rows],
-            WY + dz * 2 + way,
+            WY + (dz * 2 + way) * 2 + part,
             dev_y(1 if way == 0 else 3),
         )
+
+    def wx(dz, d):
+        piece = wother.at[(z + dz) % 4, c, pl.ds(pl.multiple_of(quarter, 32), QUARTER)]
+        return rcopy(piece, piece, WX + dz * 3 + d - 1, dev_x(d))
+
+    def wy_start(dz):
+        for way in range(2):
+            for part in range(2):
+                wy(dz, way, part).start()
+
+    def spread(dz):
+        for way in range(2):
+            for part in range(2):
+                wy(dz, way, part).wait()
+        for d in (2, 1, 3):
+            wx(dz, d).start()
+
+    def arrived(dz):
+        for d in (1, 2, 3):
+            wx(dz, d).wait()
+        ws(dz, 1).start()
 
     def ws(dz, other):
         piece = (wother if other else wsame).at[(z + dz) % 4, c]
@@ -208,8 +240,7 @@
 
     for i in range(2):
         wz(i).start()
-    for way in range(2):
-        wy(0, way).start()
+    wy_start(0)
 
     def hidden_copy(j):
         to = (f + j) % 16
@@ -237,6 +268,18 @@
     def summed(i, zz, k):
         piece = ga.at[right if i == 0 else left, i, zz]
         return rcopy(piece, r1a.at[i, i, zz], F1 + i * 4 + k, dev_x(1 if i == 0 else 3))
+
+    def b1(d, zz, k):
+        yy = (y + d) % 4
+        return rcopy(
+            gb.at[:, yy // 2, zz, yy % 2], r1b.at[d - 1, :, zz], B1 + (d - 1) * 4 + k, dev_y(d)
+        )
+
+    def b2(d):
+        return rcopy(s1b.at[:, (z + d) % 4], r2b.at[d - 1], B2 + d - 1, dev_z(d))
+
+    def b3(d):
+        return rcopy(s2b.at[(x + d) % 4], r3b.at[d - 1], B3 + d - 1, dev_x(d))
 
     def c1(d):
         return rcopy(gc.at[:, :, (z + d) % 4], r1c.at[d - 1], C1 + d - 1, dev_z(d))
@@ -288,13 +331,16 @@
             part = part.astype(bf16)
             for b in range(4):
                 xx, hh = half * 2 + b // 2, b % 2
-                ga[xx, hh, zz, ll] = part[b * 64 : (b + 1) * 64, 0:512]
+                ga[xx, hh, zz, ll] = part[b * 64 : (b + 1) * 64, 0:384]
+                gb[xx, hh, zz, ll] = part[b * 64 : (b + 1) * 64, 384:512]
                 gc[xx, hh, zz, ll] = part[b * 64 : (b + 1) * 64, 512:640]
 
         for i in range(2):
             two_hop(i, zz, k).start()
         for i in range(2):
             direct(i, zz, k).start()
+        for d in (2, 1, 3):
+            b1(d, zz, k).start()
         if k < 3:
             c1(k + 1).start()
         if k > 0:
@@ -310,8 +356,7 @@
     for i in range(2):
         wf(i).start()
     for dz in (1, 3):
-        for way in range(2):
-            wy(dz, way).start()
+        wy_start(dz)
         ws(dz, 0).start()
 
     local[5].wait()
@@ -373,8 +418,24 @@
         if k < 3:
             a3(k + 1).start()
 
+    def first_b(k):
+        zz = (z + 1 + k) % 4
+        for d in (1, 2, 3):
+            b1(d, zz, k).wait()
+
+        @pl.loop(0, 4)
+        def _(i):
+            s1b[i, zz] = total(gb[i, yh, zz, yl], r1b, (i, zz)).astype(bf16)
+
+        if k < 3:
+            b2(k + 1).start()
+
     first(0)
+    first_b(0)
     pl.loop(0, 2)(attend)
+    spread(0)
+    first(1)
+    first_b(1)
     for d in (1, 2, 3):
         c1(d).wait()
 
@@ -385,16 +446,17 @@
 
     for d in (2, 1, 3):
         c2(d).start()
-    first(1)
-    pl.loop(2, 4)(attend)
     for i in range(2):
         wf(i).wait()
-    for way in range(2):
-        wy(2, way).start()
+    wy_start(2)
     ws(2, 0).start()
+    pl.loop(2, 4)(attend)
+    first(2)
+    first_b(2)
     second(0)
-    first(2)
     input_grad(0)
+    first(3)
+    first_b(3)
     second(1)
     for d in (1, 2, 3):
         c2(d).wait()
@@ -406,18 +468,26 @@
 
     for d in (2, 1, 3):
         c3(d).start()
-    for way in range(2):
-        wy(0, way).wait()
-    ws(0, 1).start()
-    first(3)
+    for d in (1, 2, 3):
+        b2(d).wait()
+
+    @pl.loop(0, 4)
+    def _(i):
+        s2b[i] = total(s1b[i, z], r2b, (i,))
+
+    for d in (2, 1, 3):
+        b3(d).start()
+    spread(1)
+    spread(3)
     second(2)
-    input_grad(1)
     second(3)
 
     for d in (1, 2, 3):
         a3(d).wait()
+        b3(d).wait()
         c3(d).wait()
-    gx[c, :, 0:512] = total(s2a[z], r3a, ()) * grad_factor
+    gx[c, :, 0:384] = total(s2a[z], r3a, ()) * grad_factor
+    gx[c, :, 384:512] = total(s2b[x], r3b, ()) * grad_factor
     gx[c, :, 512:640] = total(s2c[yh, yl], r3c, ()) * grad_factor
     gx_copy = rcopy(gx.at[c], gx.at[c], GX, sib)
     gx_copy.start()
@@ -454,12 +524,13 @@
     def _(j):
         fresh_copy(j).start()
 
-    for dz in (1, 3, 2):
-        for way in range(2):
-            wy(dz, way).wait()
-        ws(dz, 1).start()
+    spread(2)
+    for dz in (0, 1, 3):
+        arrived(dz)
+    input_grad(1)
     input_grad(3)
     input_grad(2)
+    arrived(2)
 
     @pl.loop(1, 16)
     def _(j):
@@ -510,18 +581,24 @@
         V((320, 1024), f32),
         V((320, 128), f32),
         V((320, 128), f32),
-        V((4, 2, 4, 2, 64, 512), bf16),
+        V((4, 2, 4, 2, 64, 384), bf16),
         V((4, 2, 4, 2, 64, 128), bf16),
-        V((2, 4, 2, 64, 512), bf16),
-        V((2, 2, 4, 2, 64, 512), bf16),
+        V((4, 2, 4, 2, 64, 128), bf16),
+        V((2, 4, 2, 64, 384), bf16),
+        V((2, 2, 4, 2, 64, 384), bf16),
+        V((3, 4, 4, 64, 128), bf16),
         V((3, 4, 2, 2, 64, 128), bf16),
-        V((2, 4, 2, 64, 512), bf16),
+        V((2, 4, 2, 64, 384), bf16),
+        V((4, 4, 64, 128), bf16),
         V((4, 2, 2, 64, 128), bf16),
-        V((3, 4, 64, 512), bf16),
+        V((3, 4, 64, 384), bf16),
+        V((3, 4, 64, 128), bf16),
         V((3, 2, 2, 64, 128), bf16),
-        V((4, 64, 512), f32),
+        V((4, 64, 384), f32),
+        V((4, 64, 128), f32),
         V((2, 2, 64, 128), f32),
-        V((3, 64, 512), f32),
+        V((3, 64, 384), f32),
+        V((3, 64, 128), f32),
         V((3, 64, 128), f32),
         V((2, 64, 640), f32),
         V((640, 128), f32),

time: 113 us -> 100 us (0.88)
  Pallas kernels: 109 us -> 96.5 us
    pallas_call x1, Pallas kernels: 98.1 us -> 85.5 us  [learn(): pl.pallas_call(functools.partial(learn_kernel, grad_factor), out_shape=(s...]
where the time goes in v5:
time: 100 us
  Pallas kernels  96.5 us (96%)
  local copies, waits for them, and re-layouts  2.84 us (3%)
    pallas_call x1, Pallas kernels, learn(): pl.pallas_call(functools.partial(learn_kernel, grad_factor), out_shape=(s...  85.5 us
    pallas_call x1, Pallas kernels, finish(): pl.pallas_call(finish_kernel, grid=(4,), out_shape=(jax.ShapeDtypeStruct(...  11 us

profile of v5, /device:TPU:1, one launch (start us, length us, event | category | flops | bytes accessed | tf_op | source)
XLA Modules:
  0.0 100.0 jit_solution(7354727814271152641)
XLA Ops:
  0.6 1.6 %reshape.19.hidden = bf16[16,5120]{1,0:T(8,128)(2,1)} reshape(bf16[4,4,5120]{2,1,0:T(4,128)(2,1)} %param.16) | data formatting | bytes 327680 | tf_op jit(solution)/shard_map/reshape | solution.py:687
  2.3 85.5 %learn.1 = (bf16[4,2,320,1024]{3,2,1,0:T(8,128)(2,1)}, bf16[8,320,128]{2,1,0:T(8,128)(2,1)}, bf16[4,512,640]{2,1,0:T(8,128)(2,1)}, bf16[2,16,128]{2,1,0:T(8,128)(2,1)}, bf16[4,4,640]{2,1,0:T(4,128)(2,1)}) custom-call(bf16[512,5120]{1,0:T(8,128)(2,1)} %x_hbm.1, bf16[512,1024]{1,0:T(8,128)(2,1)} %u.3, f32[320,1024]{1,0:T(8,128)} %master.1, f32[320,1024]{1,0:T(8,128)} %m1.1, ...), custom_call_target="tpu_custom_call" | custom-call | tf_op jit(solution)/shard_map/learn/pallas_call | solution.py:614
  87.8 0.0 copy-start.1
  87.8 0.0 copy-start
  87.8 11.0 %finish.1 = (bf16[512,5120]{1,0:T(8,128)(2,1)}, f32[320,1024]{1,0:T(8,128)}, f32[320,1024]{1,0:T(8,128)}) custom-call(bf16[512,1024]{1,0:T(8,128)(2,1)} %u.3, bf16[4,512,640]{2,1,0:T(8,128)(2,1)} %get-tuple-element.13.part, bf16[2560,1024]{1,0:T(8,128)(2,1)} %bitcast.5, bf16[8,320,128]{2,1,0:T(8,128)(2,1)} %get-tuple-element.15.grad, f32[320,1024]{1,0:T(8,128)} %master.1, ...), custom_call_target="tpu_custom_call" | custom-call | tf_op jit(solution)/shard_map/finish/pallas_call | solution.py:650
  98.8 0.0 copy-done.1
  98.8 0.6 copy.18
  99.4 0.0 copy-done
  99.4 0.6 copy.20
Async XLA Ops:
  87.8 11.0 %copy-start.1 = (bf16[2,16,128]{2,1,0:T(8,128)(2,1)S(1)}, bf16[2,16,128]{2,1,0:T(8,128)(2,1)}, u32[]{:S(2)}) copy-start(bf16[2,16,128]{2,1,0:T(8,128)(2,1)} %get-tuple-element.19) | copy-start | bytes 24580
  87.8 11.6 %copy-start = (bf16[4,4,640]{2,1,0:T(4,128)(2,1)S(1)}, bf16[4,4,640]{2,1,0:T(4,128)(2,1)}, u32[]{:S(2)}) copy-start(bf16[4,4,640]{2,1,0:T(4,128)(2,1)} %get-tuple-element.30) | copy-start | bytes 61444

commit v6 on v5

--- a/solution.py
+++ b/solution.py
@@ -44,7 +44,7 @@
     master_hbm,
     m1_hbm,
     m2_hbm,
-    hidden,
+    hidden_steps,
     kw_hbm,
     queries,
     k_hbm,
@@ -55,6 +55,8 @@
     part_hbm,
     fresh_out,
     attended,
+    hidden_wide,
+    hidden,
     ut,
     wsame,
     kw,
@@ -155,6 +157,10 @@
         device_id_type=MESH,
     )
 
+    for step in range(4):
+        hidden_wide[step * 4 : (step + 1) * 4] = hidden_steps[step].astype(f32)
+    hidden[...] = hidden_wide[...].astype(bf16)
+
     for tt in range(8):
         block = u[:, tt * 128 : (tt + 1) * 128].T
         place = ((tt % 4) * 2 + tt // 4) * 64
@@ -430,57 +436,70 @@
         if k < 3:
             b2(k + 1).start()
 
+    def second_b():
+        for d in (1, 2, 3):
+            b2(d).wait()
+
+        @pl.loop(0, 4)
+        def _(i):
+            s2b[i] = total(s1b[i, z], r2b, (i,))
+
+        for d in (2, 1, 3):
+            b3(d).start()
+
+    def first_c():
+        for d in (1, 2, 3):
+            c1(d).wait()
+
+        @pl.loop(0, 16)
+        def _(i):
+            xx, hh, ll = i // 4, (i // 2) % 2, i % 2
+            s1c[xx, hh, ll] = total(gc[xx, hh, z, ll], r1c, (xx, hh, ll)).astype(bf16)
+
+        for d in (2, 1, 3):
+            c2(d).start()
+
+    def second_c():
+        for d in (1, 2, 3):
+            c2(d).wait()
+
+        @pl.loop(0, 4)
+        def _(i):
+            hh, ll = i // 2, i % 2
+            s2c[hh, ll] = total(s1c[x, hh, ll], r2c, (hh, ll))
+
+        for d in (2, 1, 3):
+            c3(d).start()
+
     first(0)
     first_b(0)
-    pl.loop(0, 2)(attend)
-    spread(0)
+    pl.loop(0, 1)(attend)
     first(1)
     first_b(1)
-    for d in (1, 2, 3):
-        c1(d).wait()
-
-    @pl.loop(0, 16)
-    def _(i):
-        xx, hh, ll = i // 4, (i // 2) % 2, i % 2
-        s1c[xx, hh, ll] = total(gc[xx, hh, z, ll], r1c, (xx, hh, ll)).astype(bf16)
-
-    for d in (2, 1, 3):
-        c2(d).start()
+    pl.loop(1, 2)(attend)
+    spread(0)
+    input_grad(0)
+    first(2)
+    first_b(2)
+    first_c()
+    second(0)
+    pl.loop(2, 3)(attend)
     for i in range(2):
         wf(i).wait()
     wy_start(2)
     ws(2, 0).start()
-    pl.loop(2, 4)(attend)
-    first(2)
-    first_b(2)
-    second(0)
-    input_grad(0)
+    pl.loop(3, 4)(attend)
     first(3)
     first_b(3)
+    input_grad(1)
     second(1)
-    for d in (1, 2, 3):
-        c2(d).wait()
-
-    @pl.loop(0, 4)
-    def _(i):
-        hh, ll = i // 2, i % 2
-        s2c[hh, ll] = total(s1c[x, hh, ll], r2c, (hh, ll))
-
-    for d in (2, 1, 3):
-        c3(d).start()
-    for d in (1, 2, 3):
-        b2(d).wait()
-
-    @pl.loop(0, 4)
-    def _(i):
-        s2b[i] = total(s1b[i, z], r2b, (i,))
-
-    for d in (2, 1, 3):
-        b3(d).start()
+    second_c()
+    second_b()
     spread(1)
     spread(3)
     second(2)
     second(3)
+    input_grad(3)
 
     for d in (1, 2, 3):
         a3(d).wait()
@@ -527,8 +546,6 @@
     spread(2)
     for dz in (0, 1, 3):
         arrived(dz)
-    input_grad(1)
-    input_grad(3)
     input_grad(2)
     arrived(2)
 
@@ -567,6 +584,8 @@
     shape = jax.ShapeDtypeStruct
     V = pltpu.VMEM
     scratch = [
+        V((16, 5120), f32),
+        V((16, 5120), bf16),
         V((2, 512, 512), bf16),
         V((4, 2, 320, 1024), bf16),
         V((5120, 128), bf16),
@@ -630,7 +649,15 @@
     )(inputs, upstream, master, m1, m2, flat, key_weight, queries, keys, values, lengths)
 
 
-def finish_kernel(u, part, w, grad, master, m1, m2, input_grad, new_master, new_moment):
+def finish_kernel(
+    u, part, w, grad, master, m1, m2, fresh, heads, input_grad, new_master, new_moment, kv, attended
+):
+    @pl.when(pl.program_id(0) == 0)
+    def _():
+        wide = fresh[...].astype(f32).reshape(2, 4, 4, 128)
+        kv[...] = jnp.stack([wide[0], wide[1]], axis=2).astype(bf16)
+        attended[...] = heads[...]
+
     yl = (lax.axis_index("fsdp") // 2) % 2
     same = pl.ds(pl.multiple_of(yl * 640, 640), 640)
     other = pl.ds(pl.multiple_of((1 - yl) * 640, 640), 640)
@@ -645,7 +672,8 @@
         )
 
 
-def finish(upstream, part, weight, grad, master, m1, m2):
+def finish(upstream, part, weight, grad, master, m1, m2, fresh, heads):
+    vmem = pl.BlockSpec(memory_space=pltpu.VMEM)
     cols = pl.BlockSpec((320, 256), lambda i: (0, i))
     return pl.pallas_call(
         finish_kernel,
@@ -654,6 +682,8 @@
             jax.ShapeDtypeStruct((512, 5120), bf16),
             jax.ShapeDtypeStruct((320, 1024), f32),
             jax.ShapeDtypeStruct((320, 1024), f32),
+            jax.ShapeDtypeStruct((4, 4, 2, 128), bf16),
+            jax.ShapeDtypeStruct((4, 4, 640), bf16),
         ),
         in_specs=[
             pl.BlockSpec((512, 1024), lambda i: (0, 0)),
@@ -663,11 +693,13 @@
             cols,
             cols,
             cols,
+            vmem,
+            vmem,
         ],
-        out_specs=[pl.BlockSpec((512, 1280), lambda i: (0, i)), cols, cols],
+        out_specs=[pl.BlockSpec((512, 1280), lambda i: (0, i)), cols, cols, vmem, vmem],
         name="finish",
         compiler_params=pltpu.CompilerParams(vmem_limit_bytes=60 << 20),
-    )(upstream, part, weight, grad, master, m1, m2)
+    )(upstream, part, weight, grad, master, m1, m2, fresh, heads)
 
 
 def shards(
@@ -684,14 +716,13 @@
     lengths,
 ):
     grad_factor = 1.0 / math.sqrt(inputs.shape[0] * lax.axis_size("fsdp") * lax.axis_size("tp"))
-    flat = hidden_steps.reshape(16, 5120)
     weight, grad, part, fresh, attended = learn(
         inputs,
         upstream,
         master,
         moment_one,
         moment_two,
-        flat,
+        hidden_steps,
         key_weight,
         queries,
         key_cache,
@@ -699,11 +730,17 @@
         lengths,
         grad_factor,
     )
-    input_grad, new_master, new_moment = finish(
-        upstream, part, weight.reshape(2560, 1024), grad, master, moment_one, moment_two
+    return finish(
+        upstream,
+        part,
+        weight.reshape(2560, 1024),
+        grad,
+        master,
+        moment_one,
+        moment_two,
+        fresh,
+        attended,
     )
-    fresh_kv = fresh.reshape(2, 4, 4, 128).transpose(1, 2, 0, 3)
-    return (input_grad, new_master, new_moment, fresh_kv, attended)
 
 
 def solution(mesh):

time: 100 us -> 95.6 us (0.956)
  local copies, waits for them, and re-layouts: 2.84 us -> 0 us
  Pallas kernels: 96.5 us -> 94.8 us
    reshape x2 -> x0, local copies, waits for them, and re-layouts: 2.23 us -> none  [the longest x1 1.62 us: shards(): flat = hidden_steps.reshape(16, 5120)]
    pallas_call x1, Pallas kernels: 85.5 us -> 83.9 us  [learn(): pl.pallas_call(functools.partial(learn_kernel, grad_factor), out_shape=(s...]
where the time goes in v6:
time: 95.6 us; the launch traced here: 95.4 us
  Pallas kernels  94.8 us (99%)
    pallas_call x1, Pallas kernels, learn(): pl.pallas_call(functools.partial(learn_kernel, grad_factor), out_shape=(s...  83.9 us
    pallas_call x1, Pallas kernels, finish(): pl.pallas_call(finish_kernel, grid=(4,), out_shape=(jax.ShapeDtypeStruct(...  10.8 us

profile of v6, /device:TPU:1, one launch (start us, length us, event | category | flops | bytes accessed | tf_op | source)
XLA Modules:
  0.0 95.4 jit_solution(10172733190293155280)
XLA Ops:
  0.6 83.9 %learn.1 = (bf16[4,2,320,1024]{3,2,1,0:T(8,128)(2,1)}, bf16[8,320,128]{2,1,0:T(8,128)(2,1)}, bf16[4,512,640]{2,1,0:T(8,128)(2,1)}, bf16[2,16,128]{2,1,0:T(8,128)(2,1)}, bf16[4,4,640]{2,1,0:T(4,128)(2,1)}) custom-call(bf16[512,5120]{1,0:T(8,128)(2,1)} %x_hbm.1, bf16[512,1024]{1,0:T(8,128)(2,1)} %u.3, f32[320,1024]{1,0:T(8,128)} %master.1, f32[320,1024]{1,0:T(8,128)} %m1.1, ...), custom_call_target="tpu_custom_call" | custom-call | tf_op jit(solution)/shard_map/learn/pallas_call | solution.py:633
  84.6 10.8 %finish.1 = (bf16[512,5120]{1,0:T(8,128)(2,1)}, f32[320,1024]{1,0:T(8,128)}, f32[320,1024]{1,0:T(8,128)}, bf16[4,4,2,128]{3,2,1,0:T(2,128)(2,1)}, bf16[4,4,640]{2,1,0:T(4,128)(2,1)}) custom-call(bf16[512,1024]{1,0:T(8,128)(2,1)} %u.3, bf16[4,512,640]{2,1,0:T(8,128)(2,1)} %get-tuple-element.10.part, bf16[2560,1024]{1,0:T(8,128)(2,1)} %bitcast.1, ...), custom_call_target="tpu_custom_call" | custom-call | tf_op jit(solution)/shard_map/finish/pallas_call | solution.py:678

commit v7 on v6

--- a/solution.py
+++ b/solution.py
@@ -355,7 +355,6 @@
             for cp in local[5:]:
                 cp.start()
             ws(0, 0).start()
-    pass_on(3)
 
     for i in range(2):
         wz(i).wait()
@@ -364,6 +363,8 @@
     for dz in (1, 3):
         wy_start(dz)
         ws(dz, 0).start()
+    pass_on(3)
+
 
     local[5].wait()
     fresh_out[0] = jnp.dot(hidden[...], kw[...], preferred_element_type=f32).astype(bf16)
@@ -499,6 +500,7 @@
     spread(3)
     second(2)
     second(3)
+    spread(2)
     input_grad(3)
 
     for d in (1, 2, 3):
@@ -543,11 +545,9 @@
     def _(j):
         fresh_copy(j).start()
 
-    spread(2)
-    for dz in (0, 1, 3):
+    for dz in (0, 1, 3, 2):
         arrived(dz)
     input_grad(2)
-    arrived(2)
 
     @pl.loop(1, 16)
     def _(j):

time: 95.6 us -> 87.4 us (0.914)
  Pallas kernels: 94.8 us -> 86.6 us
    pallas_call x1, Pallas kernels: 83.9 us -> 75.8 us  [learn(): pl.pallas_call(functools.partial(learn_kernel, grad_factor), out_shape=(s...]
where the time goes in v7:
time: 87.4 us; the launch traced here: 87.2 us
  Pallas kernels  86.6 us (99%)
    pallas_call x1, Pallas kernels, learn(): pl.pallas_call(functools.partial(learn_kernel, grad_factor), out_shape=(s...  75.8 us
    pallas_call x1, Pallas kernels, finish(): pl.pallas_call(finish_kernel, grid=(4,), out_shape=(jax.ShapeDtypeStruct(...  10.8 us

profile of v7, /device:TPU:1, one launch (start us, length us, event | category | flops | bytes accessed | tf_op | source)
XLA Modules:
  0.0 87.2 jit_solution(15727913059158464001)
XLA Ops:
  0.6 75.8 %learn.1 = (bf16[4,2,320,1024]{3,2,1,0:T(8,128)(2,1)}, bf16[8,320,128]{2,1,0:T(8,128)(2,1)}, bf16[4,512,640]{2,1,0:T(8,128)(2,1)}, bf16[2,16,128]{2,1,0:T(8,128)(2,1)}, bf16[4,4,640]{2,1,0:T(4,128)(2,1)}) custom-call(bf16[512,5120]{1,0:T(8,128)(2,1)} %x_hbm.1, bf16[512,1024]{1,0:T(8,128)(2,1)} %u.3, f32[320,1024]{1,0:T(8,128)} %master.1, f32[320,1024]{1,0:T(8,128)} %m1.1, ...), custom_call_target="tpu_custom_call" | custom-call | tf_op jit(solution)/shard_map/learn/pallas_call | solution.py:633
  76.4 10.8 %finish.1 = (bf16[512,5120]{1,0:T(8,128)(2,1)}, f32[320,1024]{1,0:T(8,128)}, f32[320,1024]{1,0:T(8,128)}, bf16[4,4,2,128]{3,2,1,0:T(2,128)(2,1)}, bf16[4,4,640]{2,1,0:T(4,128)(2,1)}) custom-call(bf16[512,1024]{1,0:T(8,128)(2,1)} %u.3, bf16[4,512,640]{2,1,0:T(8,128)(2,1)} %get-tuple-element.10.part, bf16[2560,1024]{1,0:T(8,128)(2,1)} %bitcast.1, ...), custom_call_target="tpu_custom_call" | custom-call | tf_op jit(solution)/shard_map/finish/pallas_call | solution.py:678

commit v8 on v7

--- a/solution.py
+++ b/solution.py
@@ -482,13 +482,13 @@
     input_grad(0)
     first(2)
     first_b(2)
-    first_c()
-    second(0)
-    pl.loop(2, 3)(attend)
     for i in range(2):
         wf(i).wait()
     wy_start(2)
     ws(2, 0).start()
+    first_c()
+    second(0)
+    pl.loop(2, 3)(attend)
     pl.loop(3, 4)(attend)
     first(3)
     first_b(3)

time: 87.4 us -> 88.6 us (1.014)
  Pallas kernels: 86.6 us -> 87.8 us
    pallas_call x1, Pallas kernels: 75.8 us -> 77 us  [learn(): pl.pallas_call(functools.partial(learn_kernel, grad_factor), out_shape=(s...]
where the time goes in v8:
time: 88.6 us; the launch traced here: 88.5 us
  Pallas kernels  87.8 us (99%)
    pallas_call x1, Pallas kernels, learn(): pl.pallas_call(functools.partial(learn_kernel, grad_factor), out_shape=(s...  77 us
    pallas_call x1, Pallas kernels, finish(): pl.pallas_call(finish_kernel, grid=(4,), out_shape=(jax.ShapeDtypeStruct(...  10.8 us

profile of v8, /device:TPU:1, one launch (start us, length us, event | category | flops | bytes accessed | tf_op | source)
XLA Modules:
  0.0 88.5 jit_solution(7404901180733385688)
XLA Ops:
  0.6 77.0 %learn.1 = (bf16[4,2,320,1024]{3,2,1,0:T(8,128)(2,1)}, bf16[8,320,128]{2,1,0:T(8,128)(2,1)}, bf16[4,512,640]{2,1,0:T(8,128)(2,1)}, bf16[2,16,128]{2,1,0:T(8,128)(2,1)}, bf16[4,4,640]{2,1,0:T(4,128)(2,1)}) custom-call(bf16[512,5120]{1,0:T(8,128)(2,1)} %x_hbm.1, bf16[512,1024]{1,0:T(8,128)(2,1)} %u.3, f32[320,1024]{1,0:T(8,128)} %master.1, f32[320,1024]{1,0:T(8,128)} %m1.1, ...), custom_call_target="tpu_custom_call" | custom-call | tf_op jit(solution)/shard_map/learn/pallas_call | solution.py:633
  77.6 10.8 %finish.1 = (bf16[512,5120]{1,0:T(8,128)(2,1)}, f32[320,1024]{1,0:T(8,128)}, f32[320,1024]{1,0:T(8,128)}, bf16[4,4,2,128]{3,2,1,0:T(2,128)(2,1)}, bf16[4,4,640]{2,1,0:T(4,128)(2,1)}) custom-call(bf16[512,1024]{1,0:T(8,128)(2,1)} %u.3, bf16[4,512,640]{2,1,0:T(8,128)(2,1)} %get-tuple-element.10.part, bf16[2560,1024]{1,0:T(8,128)(2,1)} %bitcast.1, ...), custom_call_target="tpu_custom_call" | custom-call | tf_op jit(solution)/shard_map/finish/pallas_call | solution.py:678
